TPU v7x, 128 devices: a whole 4x4x4 slice. The times are simulated.
128 devices in a mesh: gx: 16 (over z, y), gy: 8 (over x, core).
Axes of the slice: x: 4, y: 4, z: 4, core: 2. Of those that a mesh axis runs over, the one named last changes fastest.
Arguments:
- user_table: float32 [524288, 128], P(('gx', 'gy'))
- item_table: float32 [524288, 128], P(('gx', 'gy'))
- item_owner: int32 [786432, 1], P(('gx', 'gy')), may hold values from 0 to 127; in each aligned block of 6144 rows (0 to 6143, 6144 to 12287, ...) at most 60 rows name the same one
- item_row: int32 [786432], P(('gx', 'gy')), may hold values from 0 to 4095
- user_confidence: float32 [786432], P(('gx', 'gy')), may hold values from 0.5 to 8
- user_rating: float32 [786432], P(('gx', 'gy')), may hold values from -12 to 12
- user_counts: int32 [6144, 4], P(('gx', 'gy')), may hold values from 1 to 64, 112 in all within a row
- user_owner: int32 [786432, 1], P(('gx', 'gy')), may hold values from 0 to 127; in each aligned block of 6144 rows (0 to 6143, 6144 to 12287, ...) at most 60 rows name the same one
- user_row: int32 [786432], P(('gx', 'gy')), may hold values from 0 to 4095
- item_confidence: float32 [786432], P(('gx', 'gy')), may hold values from 0.5 to 8
- item_rating: float32 [786432], P(('gx', 'gy')), may hold values from -12 to 12
- item_counts: int32 [6144, 4], P(('gx', 'gy')), may hold values from 1 to 64, 112 in all within a row
Outputs:
- new_users: float32 [524288, 128], P(('gx', 'gy'))
- new_items: float32 [524288, 128], P(('gx', 'gy'))
Inputs may be any that keep to these rules, and one draw needn't show every extreme that they name: `item_owner`: among the 6144 slots of one device at most 60 name the same owner, a bound that some block reaches. `user_owner`: among the 6144 slots of one device at most 60 name the same owner, a bound that some block reaches. `user_counts`: each row of 4 counts sums to 112. `item_counts`: each row of 4 counts sums to 112.
All inputs are finite; a program needn't handle non-finite values.
Results may differ from a plain program's by a relative error of at most 0.024.
The roundings to bfloat16 on the way count: a program that leaves them out, or rounds other values in their place, can miss the bound.
Values may be sent and summed in bfloat16 or wider, within the bound.
No kernel may reach another device: no remote copies, remote signals or barrier semaphores. Data moves between devices by JAX's collectives and lax.ppermute only.
A program may use at most 128 MiB of HBM per device.

v0:
```python
import jax
import jax.numpy as jnp
from jax import lax
from jax.sharding import PartitionSpec as P

ITERS = 8


ridge_weight = 1.0
global_weight = 256.0
guard_eps = 1e-06


def apply_system(system, vector):
    return jnp.einsum("bkl,bl->bk", system, vector, precision=lax.Precision.HIGHEST)


def conjugate(system, right_side, warm_start):
    iterate = warm_start
    resid = right_side - apply_system(system, iterate)
    direction = resid
    norm_now = jnp.sum(resid * resid, -1, keepdims=True)
    for iteration in range(ITERS):
        images = apply_system(system, direction)
        step_size = norm_now / (jnp.sum(direction * images, -1, keepdims=True) + guard_eps)
        iterate = iterate + step_size * direction
        resid = resid - step_size * images
        norm_next = jnp.sum(resid * resid, -1, keepdims=True)
        direction = resid + norm_next / (norm_now + guard_eps) * direction
        norm_now = norm_next
    return iterate


def solve_blocks(fetched, confidence, rating, counts, warm_start, global_gram, gram_scale):
    block_count, block_rows, width = fetched.shape
    seg_ends = jnp.cumsum(counts, -1, dtype=jnp.int32)
    begins = seg_ends - counts
    position = jnp.arange(block_rows, dtype=jnp.int32)
    inside = (position[None, None, :] >= begins[..., None]) & (
        position[None, None, :] < seg_ends[..., None]
    )
    weights = jnp.where(inside, confidence[:, None, :], jnp.zeros((), confidence.dtype))
    weighted = (weights[..., None] * fetched[:, None]).astype(jnp.bfloat16)
    local_gram = jnp.einsum("bsjk,bjl->bskl", weighted, fetched, preferred_element_type=jnp.float32)
    right_side = jnp.einsum(
        "bsj,bjk->bsk",
        weights * rating[:, None, :],
        fetched.astype(jnp.float32),
        precision=lax.Precision.HIGHEST,
    )
    system = (
        ridge_weight * jnp.eye(width, dtype=jnp.float32) + gram_scale * global_gram + local_gram
    )
    solved = conjugate(
        system.reshape(-1, width, width),
        right_side.reshape(-1, width),
        warm_start.reshape(-1, width),
    )
    return solved.reshape(block_count, -1, width)


def fetch_rows(source_narrow, owner, rows_local):
    devices = lax.axis_size(("gx", "gy"))
    slot_count = owner.shape[0]
    width = source_narrow.shape[1]
    capacity = 5 * slot_count // (4 * devices)
    sorted_order = jnp.argsort(owner, stable=True)
    sorted_owner = owner[sorted_order]
    per_owner = jnp.sum(
        (owner[:, None] == jnp.arange(devices, dtype=jnp.int32)[None, :]).astype(jnp.int32), 0
    )
    owner_starts = jnp.cumsum(per_owner) - per_owner
    rank_sorted = jnp.arange(slot_count, dtype=jnp.int32) - owner_starts[sorted_owner]
    bucket_rank = jnp.zeros((slot_count,), jnp.int32).at[sorted_order].set(rank_sorted)
    send_slot = owner * capacity + bucket_rank
    requests = jnp.zeros((devices * capacity,), jnp.int32).at[send_slot].set(rows_local)
    row_values = source_narrow[
        lax.all_to_all(
            requests.reshape(devices, capacity),
            ("gx", "gy"),
            split_axis=0,
            concat_axis=0,
            tiled=True,
        )
    ]
    replies = lax.all_to_all(row_values, ("gx", "gy"), split_axis=0, concat_axis=0, tiled=True)
    return replies.reshape(devices * capacity, width)[send_slot]


def half_step(own_table, source, owner, rows_local, confidence, rating, counts):
    devices = lax.axis_size(("gx", "gy"))
    tab_rows, width = own_table.shape
    block_count, per_block = counts.shape
    block_rows = owner.shape[0] // block_count
    batch_rows = block_count * per_block
    local_gram = jnp.dot(
        source.T, source, precision=lax.Precision.HIGHEST, preferred_element_type=jnp.float32
    )
    global_gram = lax.psum(local_gram, ("gx", "gy"))
    gram_scale = global_weight / (tab_rows * devices)
    fetched = fetch_rows(source.astype(jnp.bfloat16), owner[:, 0], rows_local)
    renewed = solve_blocks(
        fetched.reshape(block_count, block_rows, width),
        confidence.reshape(block_count, block_rows),
        rating.reshape(block_count, block_rows),
        counts,
        own_table[:batch_rows].reshape(block_count, per_block, width),
        global_gram,
        gram_scale,
    )
    return jnp.concatenate([renewed.reshape(batch_rows, width), own_table[batch_rows:]], 0)


def shards(
    user_table,
    item_table,
    item_owner,
    item_row,
    user_confidence,
    user_rating,
    user_counts,
    user_owner,
    user_row,
    item_confidence,
    item_rating,
    item_counts,
):
    new_users = half_step(
        user_table, item_table, item_owner, item_row, user_confidence, user_rating, user_counts
    )
    new_items = half_step(
        item_table, new_users, user_owner, user_row, item_confidence, item_rating, item_counts
    )
    return (new_users, new_items)


def solution(mesh):
    in_specs = (
        P(("gx", "gy"), None),
        P(("gx", "gy"), None),
        P(("gx", "gy"), None),
        P(("gx", "gy")),
        P(("gx", "gy")),
        P(("gx", "gy")),
        P(("gx", "gy"), None),
        P(("gx", "gy"), None),
        P(("gx", "gy")),
        P(("gx", "gy")),
        P(("gx", "gy")),
        P(("gx", "gy"), None),
    )
    out_specs = (P(("gx", "gy"), None), P(("gx", "gy"), None))
    return jax.shard_map(shards, mesh=mesh, in_specs=in_specs, out_specs=out_specs, check_vma=False)
```

profile of v0, /device:TPU:1, one launch (start us, length us, event | category | flops | bytes accessed | tf_op | source)
XLA Modules:
  0.0 1082.6 jit_solution(14641948129178718111)
XLA Ops:
  7.2 3.2 convert_reduce_fusion.1
  10.8 7.4 sort.31
  18.3 34.3 %gather_fusion = s32[6144]{0:T(1024)S(1)} fusion(s32[6144]{0:T(1024)S(1)} %bitcast.170, s32[6144]{0:T(1024)S(1)} %get-tuple-element.38), kind=kCustom, calls=%fused_computation | custom fusion | bytes 73728 | tf_op jit(solution)/shard_map/gather | solution.py:68
  52.7 36.8 %gather_fusion.1 = s32[6144]{0:T(1024)S(1)} fusion(s32[128]{0:T(128)S(1)} %sub.67, s32[6144]{0:T(1024)S(1)} %broadcast_clamp_fusion.3), kind=kCustom, calls=%fused_computation.1 | custom fusion | bytes 73728 | tf_op jit(solution)/shard_map/gather | solution.py:73
  89.5 23.0 %scatter_custom_fusion = s32[6144]{0:T(1024)S(1)} fusion(s32[6144]{0:T(1024)S(1)} %get-tuple-element.39, s32[6144]{0:T(1024)S(1)} %iota_subtract_fusion.1, s32[]{:T(128)} %constant.9.clone.1), kind=kCustom, calls=%fused_computation.131 | custom fusion | bytes 24580 | tf_op jit(solution)/shard_map/scatter | solution.py:74
  112.5 23.2 %scatter_custom_fusion.1 = s32[7680]{0:T(1024)S(1)} fusion(s32[6144]{0:T(1024)S(1)} %get-tuple-element.35, s32[6144]{0:T(1024)} %param.15, s32[]{:T(128)} %constant.9.clone.1), kind=kCustom, calls=%fused_computation.121 | custom fusion | bytes 31232 | tf_op jit(solution)/shard_map/scatter | solution.py:76
  136.5 11.8 %all-to-all-start = ((s32[128,1,60]{2,1,0:T(1,128)}), s32[128,1,60]{2,1,0:T(1,128)S(1)}, u32[]{:S(2)}, u32[]{:S(2)}) async-start(s32[128,1,60]{2,1,0:T(1,128)} %bitcast.6), calls=%async_computation | async-start | bytes 131072 | tf_op jit(solution)/shard_map/all_to_all | solution.py:78
  148.3 2.7 convert_reduce_fusion
  151.4 6.7 sort.32
  158.2 34.3 %gather_fusion.4 = s32[6144]{0:T(1024)S(1)} fusion(s32[6144]{0:T(1024)S(1)} %bitcast.174, s32[6144]{0:T(1024)S(1)} %get-tuple-element.36), kind=kCustom, calls=%fused_computation.4 | custom fusion | bytes 73728 | tf_op jit(solution)/shard_map/gather | solution.py:68
  192.5 36.8 %gather_fusion.5 = s32[6144]{0:T(1024)S(1)} fusion(s32[128]{0:T(128)S(1)} %sub.78, s32[6144]{0:T(1024)S(1)} %broadcast_clamp_fusion.2), kind=kCustom, calls=%fused_computation.5 | custom fusion | bytes 73728 | tf_op jit(solution)/shard_map/gather | solution.py:73
  229.3 23.0 %scatter_custom_fusion.2 = s32[6144]{0:T(1024)S(1)} fusion(s32[6144]{0:T(1024)S(1)} %get-tuple-element.37, s32[6144]{0:T(1024)S(1)} %iota_subtract_fusion, s32[]{:T(128)} %constant.9.clone.1), kind=kCustom, calls=%fused_computation.129 | custom fusion | bytes 24580 | tf_op jit(solution)/shard_map/scatter | solution.py:74
  252.5 23.2 %scatter_custom_fusion.3 = s32[7680]{0:T(1024)S(1)} fusion(s32[6144]{0:T(1024)S(1)} %get-tuple-element.21, s32[6144]{0:T(1024)} %param.20, s32[]{:T(128)} %constant.9.clone.1), kind=kCustom, calls=%fused_computation.119 | custom fusion | bytes 31232 | tf_op jit(solution)/shard_map/scatter | solution.py:76
  276.4 9.8 all-to-all-start.2
  286.4 16.3 %gather_fusion.2 = bf16[7680,128]{1,0:T(8,128)(2,1)} fusion(bf16[4096,128]{1,0:T(8,128)(2,1)S(1)} %convert_element_type.42, s32[8192]{0:T(1024)S(1)} %pad_clamp_fusion.1), kind=kCustom, calls=%fused_computation.2 | custom fusion | bytes 3962880 | tf_op jit(solution)/shard_map/gather | solution.py:77
  302.7 3.8 reshape.479
  306.5 10.2 all-to-all-start.1
  316.8 4.1 fusion.27
  321.9 145.0 %all-reduce.3.cloned.1.call-done = f32[128,128]{1,0:T(8,128)} async-done(((f32[128,128]{1,0:T(8,128)}), f32[128,128]{1,0:T(8,128)}) %all-reduce.3.cloned.1.call-update) | async-done | bytes 65552 | tf_op jit(solution)/shard_map/psum | solution.py:99
  467.8 2.7 reshape.452
  470.5 22.3 %gather_fusion.3 = bf16[6144,128]{1,0:T(8,128)(2,1)} fusion(bf16[7680,128]{1,0:T(8,128)(2,1)S(1)} %reshape.452, s32[6144]{0:T(1024)S(1)} %get-tuple-element.34), kind=kCustom, calls=%fused_computation.3 | custom fusion | bytes 3170304 | tf_op jit(solution)/shard_map/gather | solution.py:87
  494.5 2.9 fusion.8
  499.3 19.7 %fusion.28 = f32[192,1,128]{2,1,0:T(1,128)S(1)} fusion(f32[192,128,128]{2,1,0:T(8,128)S(1)} %bitcast.176, f32[192,128,1]{1,2,0:T(1,128)S(1)} %bitcast.201), kind=kOutput, calls=%fused_computation.165 | convolution fusion | flops 37748736 | bytes 12779520 | tf_op jit(solution)/shard_map/bkl,bl->bk/dot_general | solution.py:15
  519.0 20.1 %fusion.29 = f32[192,1,128]{2,1,0:T(1,128)S(1)} fusion(f32[192,128,128]{2,1,0:T(8,128)S(1)} %bitcast.177, f32[192,128,1]{1,2,0:T(1,128)S(1)} %bitcast.202), kind=kOutput, calls=%fused_computation.166 | convolution fusion | flops 37748736 | bytes 12779520 | tf_op jit(solution)/shard_map/bkl,bl->bk/dot_general | solution.py:15
  539.6 19.9 %fusion.30 = f32[192,1,128]{2,1,0:T(1,128)S(1)} fusion(f32[192,128,128]{2,1,0:T(8,128)S(1)} %bitcast.178, f32[192,128,1]{1,2,0:T(1,128)S(1)} %bitcast.212), kind=kOutput, calls=%fused_computation.167 | convolution fusion | flops 37748736 | bytes 12779520 | tf_op jit(solution)/shard_map/bkl,bl->bk/dot_general | solution.py:15
  559.9 19.9 %fusion.31 = f32[192,1,128]{2,1,0:T(1,128)S(1)} fusion(f32[192,128,128]{2,1,0:T(8,128)S(1)} %bitcast.179, f32[192,128,1]{1,2,0:T(1,128)S(1)} %bitcast.214), kind=kOutput, calls=%fused_computation.168 | convolution fusion | flops 37748736 | bytes 12779520 | tf_op jit(solution)/shard_map/bkl,bl->bk/dot_general | solution.py:15
  580.2 19.9 %fusion.32 = f32[192,1,128]{2,1,0:T(1,128)S(1)} fusion(f32[192,128,128]{2,1,0:T(8,128)S(1)} %bitcast.180, f32[192,128,1]{1,2,0:T(1,128)S(1)} %bitcast.216), kind=kOutput, calls=%fused_computation.169 | convolution fusion | flops 37748736 | bytes 12779520 | tf_op jit(solution)/shard_map/bkl,bl->bk/dot_general | solution.py:15
  600.6 20.0 %fusion.33 = f32[192,1,128]{2,1,0:T(1,128)S(1)} fusion(f32[192,128,128]{2,1,0:T(8,128)S(1)} %bitcast.181, f32[192,128,1]{1,2,0:T(1,128)S(1)} %bitcast.218), kind=kOutput, calls=%fused_computation.170 | convolution fusion | flops 37748736 | bytes 12779520 | tf_op jit(solution)/shard_map/bkl,bl->bk/dot_general | solution.py:15
  621.1 20.2 %fusion.34 = f32[192,1,128]{2,1,0:T(1,128)S(1)} fusion(f32[192,128,128]{2,1,0:T(8,128)S(1)} %bitcast.182, f32[192,128,1]{1,2,0:T(1,128)S(1)} %bitcast.220), kind=kOutput, calls=%fused_computation.171 | convolution fusion | flops 37748736 | bytes 12779520 | tf_op jit(solution)/shard_map/bkl,bl->bk/dot_general | solution.py:15
  641.7 19.9 %fusion.35 = f32[192,1,128]{2,1,0:T(1,128)S(1)} fusion(f32[192,128,128]{2,1,0:T(8,128)S(1)} %bitcast.183, f32[192,128,1]{1,2,0:T(1,128)S(1)} %bitcast.222), kind=kOutput, calls=%fused_computation.172 | convolution fusion | flops 37748736 | bytes 12779520 | tf_op jit(solution)/shard_map/bkl,bl->bk/dot_general | solution.py:15
  662.1 19.9 %fusion.36 = f32[192,1,128]{2,1,0:T(1,128)S(1)} fusion(f32[192,128,128]{2,1,0:T(8,128)S(1)} %bitcast.184, f32[192,128,1]{1,2,0:T(1,128)S(1)} %bitcast.230), kind=kOutput, calls=%fused_computation.173 | convolution fusion | flops 37748736 | bytes 12779520 | tf_op jit(solution)/shard_map/bkl,bl->bk/dot_general | solution.py:15
  682.6 16.2 %gather_fusion.6 = bf16[7680,128]{1,0:T(8,128)(2,1)} fusion(bf16[4096,128]{1,0:T(8,128)(2,1)S(1)} %get-tuple-element.22, s32[8192]{0:T(1024)S(1)} %pad_clamp_fusion), kind=kCustom, calls=%fused_computation.6 | custom fusion | bytes 3962880 | tf_op jit(solution)/shard_map/gather | solution.py:77
  698.9 3.8 reshape.511
  702.7 5.6 all-to-all-start.3
  708.5 4.1 fusion.37
  712.8 145.7 %all-reduce.5.cloned.1.call-done = f32[128,128]{1,0:T(8,128)} async-done(((f32[128,128]{1,0:T(8,128)}), f32[128,128]{1,0:T(8,128)}) %all-reduce.5.cloned.1.call-update) | async-done | bytes 65552 | tf_op jit(solution)/shard_map/psum | solution.py:99
  859.4 2.7 reshape.458
  862.1 22.3 %gather_fusion.7 = bf16[6144,128]{1,0:T(8,128)(2,1)} fusion(bf16[7680,128]{1,0:T(8,128)(2,1)S(1)} %reshape.458, s32[6144]{0:T(1024)S(1)} %get-tuple-element.20), kind=kCustom, calls=%fused_computation.7 | custom fusion | bytes 3170304 | tf_op jit(solution)/shard_map/gather | solution.py:87
  886.1 2.9 fusion.6
  890.9 19.7 %fusion.38 = f32[192,1,128]{2,1,0:T(1,128)S(1)} fusion(f32[192,128,128]{2,1,0:T(8,128)S(1)} %bitcast.185, f32[192,128,1]{1,2,0:T(1,128)S(1)} %bitcast.194), kind=kOutput, calls=%fused_computation.175 | convolution fusion | flops 37748736 | bytes 12779520 | tf_op jit(solution)/shard_map/bkl,bl->bk/dot_general | solution.py:15
  910.6 20.1 %fusion.39 = f32[192,1,128]{2,1,0:T(1,128)S(1)} fusion(f32[192,128,128]{2,1,0:T(8,128)S(1)} %bitcast.186, f32[192,128,1]{1,2,0:T(1,128)S(1)} %bitcast.203), kind=kOutput, calls=%fused_computation.176 | convolution fusion | flops 37748736 | bytes 12779520 | tf_op jit(solution)/shard_map/bkl,bl->bk/dot_general | solution.py:15
  931.2 19.9 %fusion.40 = f32[192,1,128]{2,1,0:T(1,128)S(1)} fusion(f32[192,128,128]{2,1,0:T(8,128)S(1)} %bitcast.187, f32[192,128,1]{1,2,0:T(1,128)S(1)} %bitcast.213), kind=kOutput, calls=%fused_computation.177 | convolution fusion | flops 37748736 | bytes 12779520 | tf_op jit(solution)/shard_map/bkl,bl->bk/dot_general | solution.py:15
  951.6 19.9 %fusion.41 = f32[192,1,128]{2,1,0:T(1,128)S(1)} fusion(f32[192,128,128]{2,1,0:T(8,128)S(1)} %bitcast.188, f32[192,128,1]{1,2,0:T(1,128)S(1)} %bitcast.215), kind=kOutput, calls=%fused_computation.178 | convolution fusion | flops 37748736 | bytes 12779520 | tf_op jit(solution)/shard_map/bkl,bl->bk/dot_general | solution.py:15
  971.9 19.9 %fusion.42 = f32[192,1,128]{2,1,0:T(1,128)S(1)} fusion(f32[192,128,128]{2,1,0:T(8,128)S(1)} %bitcast.189, f32[192,128,1]{1,2,0:T(1,128)S(1)} %bitcast.217), kind=kOutput, calls=%fused_computation.179 | convolution fusion | flops 37748736 | bytes 12779520 | tf_op jit(solution)/shard_map/bkl,bl->bk/dot_general | solution.py:15
  992.3 20.0 %fusion.43 = f32[192,1,128]{2,1,0:T(1,128)S(1)} fusion(f32[192,128,128]{2,1,0:T(8,128)S(1)} %bitcast.190, f32[192,128,1]{1,2,0:T(1,128)S(1)} %bitcast.219), kind=kOutput, calls=%fused_computation.180 | convolution fusion | flops 37748736 | bytes 12779520 | tf_op jit(solution)/shard_map/bkl,bl->bk/dot_general | solution.py:15
  1012.7 20.2 %fusion.44 = f32[192,1,128]{2,1,0:T(1,128)S(1)} fusion(f32[192,128,128]{2,1,0:T(8,128)S(1)} %bitcast.191, f32[192,128,1]{1,2,0:T(1,128)S(1)} %bitcast.221), kind=kOutput, calls=%fused_computation.181 | convolution fusion | flops 37748736 | bytes 12779520 | tf_op jit(solution)/shard_map/bkl,bl->bk/dot_general | solution.py:15
  1033.4 19.9 %fusion.45 = f32[192,1,128]{2,1,0:T(1,128)S(1)} fusion(f32[192,128,128]{2,1,0:T(8,128)S(1)} %bitcast.192, f32[192,128,1]{1,2,0:T(1,128)S(1)} %bitcast.223), kind=kOutput, calls=%fused_computation.182 | convolution fusion | flops 37748736 | bytes 12779520 | tf_op jit(solution)/shard_map/bkl,bl->bk/dot_general | solution.py:15
  1053.7 19.9 %fusion.46 = f32[192,1,128]{2,1,0:T(1,128)S(1)} fusion(f32[192,128,128]{2,1,0:T(8,128)S(1)} %bitcast.193, f32[192,128,1]{1,2,0:T(1,128)S(1)} %bitcast.231), kind=kOutput, calls=%fused_computation.183 | convolution fusion | flops 37748736 | bytes 12779520 | tf_op jit(solution)/shard_map/bkl,bl->bk/dot_general | solution.py:15
  (169 shorter events, 21.9 us)
Async XLA Ops:
  7.2 11.1 %copy-start = (s32[6144,1]{0,1:T(1,128)S(1)}, s32[6144,1]{0,1:T(1,128)}, u32[]{:S(2)}) copy-start(s32[6144,1]{0,1:T(1,128)} %param.14) | copy-start | bytes 73732
  52.6 95.6 %copy-start.1 = (s32[6144,1]{0,1:T(1,128)S(1)}, s32[6144,1]{0,1:T(1,128)}, u32[]{:S(2)}) copy-start(s32[6144,1]{0,1:T(1,128)} %param.19) | copy-start | bytes 73732
  136.5 140.0 %all-to-all-start = ((s32[128,1,60]{2,1,0:T(1,128)}), s32[128,1,60]{2,1,0:T(1,128)S(1)}, u32[]{:S(2)}, u32[]{:S(2)}) async-start(s32[128,1,60]{2,1,0:T(1,128)} %bitcast.6), calls=%async_computation | async-start | bytes 131072 | tf_op jit(solution)/shard_map/all_to_all | solution.py:78
  192.5 59.9 %copy-start.2 = (f32[4096,128]{1,0:T(8,128)S(1)}, f32[4096,128]{1,0:T(8,128)}, u32[]{:S(2)}) copy-start(f32[4096,128]{1,0:T(8,128)} %param.13) | copy-start | bytes 6291460
  276.4 30.0 %all-to-all-start.2 = ((s32[128,1,60]{2,1,0:T(1,128)}), s32[128,1,60]{2,1,0:T(1,128)S(1)}, u32[]{:S(2)}, u32[]{:S(2)}) async-start(s32[128,1,60]{2,1,0:T(1,128)} %bitcast.55), calls=%async_computation.2 | async-start | bytes 131072 | tf_op jit(solution)/shard_map/all_to_all | solution.py:78
  306.5 161.3 %all-to-all-start.1 = ((bf16[128,60,128]{2,1,0:T(8,128)(2,1)}), bf16[128,60,128]{2,1,0:T(8,128)(2,1)}, u32[]{:S(2)}, u32[]{:S(2)}) async-start(bf16[128,60,128]{2,1,0:T(8,128)(2,1)} %reshape.479), calls=%async_computation.1 | async-start | bytes 4194304 | tf_op jit(solution)/shard_map/all_to_all | solution.py:86
  316.7 4.2 copy-start.10
  316.7 150.2 %all-reduce.3.cloned.1.call-start = ((), (), s32[]{:S(2)}) async-start(), calls=%async_computation.4 | async-start | bytes 131072 | tf_op jit(solution)/shard_map/psum | solution.py:99
  320.9 0.7 copy-start.8
  492.8 1.7 copy-start.12
  494.5 2.9 copy-start.4
  497.4 1.8 slice-start.2
  662.1 20.1 %copy-start.7 = (f32[4096,128]{1,0:T(8,128)S(1)}, f32[4096,128]{1,0:T(8,128)}, u32[]{:S(2)}) copy-start(f32[4096,128]{1,0:T(8,128)} %param.12) | copy-start | bytes 6291460
  662.1 20.3 %slice-start.3 = ((f32[4096,128]{1,0:T(8,128)}), f32[3904,128]{1,0:T(8,128)S(1)}, s32[]{:S(2)}) async-start(f32[4096,128]{1,0:T(8,128)} %param.12), calls=%async_computation.9 | async-start | bytes 3997696 | tf_op jit(solution)/shard_map/slice | solution.py:111
  682.6 25.9 %copy-start.6 = (f32[4096,128]{1,0:T(8,128)}, f32[4096,128]{1,0:T(8,128)S(1)}, u32[]{:S(2)}) copy-start(f32[4096,128]{1,0:T(8,128)S(1)} %get-tuple-element.23) | copy-start | bytes 6291460
  698.9 9.5 copy-start.11
  702.7 156.7 %all-to-all-start.3 = ((bf16[128,60,128]{2,1,0:T(8,128)(2,1)}), bf16[128,60,128]{2,1,0:T(8,128)(2,1)}, u32[]{:S(2)}, u32[]{:S(2)}) async-start(bf16[128,60,128]{2,1,0:T(8,128)(2,1)} %reshape.511), calls=%async_computation.3 | async-start | bytes 4194304 | tf_op jit(solution)/shard_map/all_to_all | solution.py:86
  708.2 4.4 copy-start.9
  708.3 150.2 %all-reduce.5.cloned.1.call-start = ((), (), s32[]{:S(2)}) async-start(), calls=%async_computation.5 | async-start | bytes 131072 | tf_op jit(solution)/shard_map/psum | solution.py:99
  884.4 1.7 copy-start.13
  886.1 2.9 copy-start.5
  889.0 1.8 slice-start
  1053.7 20.1 %copy-start.3 = (f32[4096,128]{1,0:T(8,128)S(1)}, f32[4096,128]{1,0:T(8,128)}, u32[]{:S(2)}) copy-start(f32[4096,128]{1,0:T(8,128)} %param.13) | copy-start | bytes 6291460
  1053.7 20.3 %slice-start.1 = ((f32[4096,128]{1,0:T(8,128)}), f32[3904,128]{1,0:T(8,128)S(1)}, s32[]{:S(2)}) async-start(f32[4096,128]{1,0:T(8,128)} %param.13), calls=%async_computation.7 | async-start | bytes 3997696 | tf_op jit(solution)/shard_map/slice | solution.py:111
Sparse Core Ops, SparseCore 0:
  322.9 144.0 all-reduce.2
  714.5 143.9 all-reduce.4
where the time goes:
time: 1090 us; the launch traced here: 1080 us
  matrix products  376 us (34%)
  local copies, waits for them, and re-layouts  331 us (30%)
  waiting for transfers between devices  291 us (27%)
  starting transfers between devices  37.4 us (3%)
  other arithmetic  32 us (3%)
  between operations  15.1 us (1%)
    dot_general x18, matrix products, apply_system(): jnp.einsum('bkl,bl->bk', system, vector, precision=lax.Precision.HIGHEST)  359 us
    psum x2, waiting for transfers between devices, half_step(): global_gram = lax.psum(local_gram, ('gx', 'gy'))  291 us
    gather x2, local copies, waits for them, and re-layouts, fetch_rows(): owner_starts[sorted_owner]  73.6 us
    gather x2, local copies, waits for them, and re-layouts, fetch_rows(): sorted_owner = owner[sorted_order]  68.6 us
    scatter x2, local copies, waits for them, and re-layouts, fetch_rows(): jnp.zeros((devices * capacity,), jnp.int32).at[send_slot].set(rows_local)  46.4 us
    scatter x2, local copies, waits for them, and re-layouts, fetch_rows(): jnp.zeros((slot_count,), jnp.int32).at[sorted_order].set(rank_sorted)  46 us
    gather x2, local copies, waits for them, and re-layouts, fetch_rows(): return replies.reshape(devices * capacity, width)[send_slot]  44.5 us
    gather x4, local copies, waits for them, and re-layouts, fetch_rows(): source_narrow[lax.all_to_all(requests.reshape(devices, capacity), ('gx',...  40.2 us
  transfers between devices with their start and end apart: 6, of which 2 were waited for; matrix products, arithmetic and copies ran while one was open for 15% of the time, Pallas kernels for 0%

commit v1 on v0

v1 whole, which is shorter than its diff:
```python
import functools

import jax
import jax.numpy as jnp
from jax import lax
from jax.experimental import pallas as pl
from jax.experimental.pallas import tpu as pltpu
from jax.sharding import PartitionSpec as P

ITERS = 8
AXES = ("gx", "gy")
LIVE = 112
PAD = 64
CAP = 60
LANES = 128

ridge_weight = 1.0
global_weight = 256.0
guard_eps = 1e-06


def bucket_kernel(chunks, owner_ref, row_ref, request_ref, slot_ref):
    sub = lax.broadcasted_iota(jnp.int32, (LANES, LANES), 0)
    lane = lax.broadcasted_iota(jnp.int32, (LANES, LANES), 1)
    below = jnp.where(sub < lane, 1.0, 0.0)
    prefix = jnp.concatenate([below, jnp.ones_like(below)], 1).astype(jnp.bfloat16)
    place = sub % PAD
    first_half = sub < PAD
    group = 8
    halves = []
    for half in range(2):

        def step(g, state):
            carry, wanted = state
            start = pl.multiple_of(half * chunks + g * group, group)
            owners = owner_ref[pl.ds(start, group), :]
            rows = row_ref[pl.ds(start, group), :]
            live = lax.broadcasted_iota(jnp.int32, owners.shape, 1) < LIVE
            masked = jnp.where(live, owners, -1)
            high = (rows // PAD).astype(jnp.float32)
            low = (rows % PAD).astype(jnp.float32)
            if half == 1:
                high, low = low, high
            hot = []
            counted = []
            for c in range(group):
                hit = sub == masked[c : c + 1, :]
                hot.append(jnp.where(hit, 1.0, 0.0))
                counted.append(
                    jnp.dot(hot[c].astype(jnp.bfloat16), prefix, preferred_element_type=jnp.float32)
                )
            ranks = []
            for c in range(group):
                before = counted[c][:, :LANES] + carry
                ranks.append(jnp.sum(before * hot[c], 0, keepdims=True).astype(jnp.int32))
                carry = carry + counted[c][:, LANES:]
            for c in range(group):
                value = jnp.where(first_half, high[c : c + 1, :], low[c : c + 1, :])
                put = jnp.where(place == ranks[c], value, 0.0).astype(jnp.bfloat16)
                wanted = wanted + lax.dot_general(
                    hot[c].astype(jnp.bfloat16),
                    put,
                    (((1,), (1,)), ((), ())),
                    preferred_element_type=jnp.float32,
                )
            slot_ref[pl.ds(start, group), :] = owners * PAD + jnp.concatenate(ranks, 0)
            return carry, wanted

        zero = jnp.zeros((LANES, LANES), jnp.float32)
        _, wanted = lax.fori_loop(0, chunks // group, step, (zero, zero))
        halves.append(wanted * PAD + pltpu.roll(wanted, PAD, 1))
    request_ref[...] = jnp.where(lane < PAD, halves[0], halves[1])


def bucket(owner, rows):
    chunks = owner.shape[0] // 2
    return pl.pallas_call(
        functools.partial(bucket_kernel, chunks),
        out_shape=(
            jax.ShapeDtypeStruct((LANES, LANES), jnp.float32),
            jax.ShapeDtypeStruct(owner.shape, jnp.int32),
        ),
        compiler_params=pltpu.CompilerParams(vmem_limit_bytes=32 << 20),
        name="bucket",
    )(owner, rows)


def gather_kernel(half, per_step, request_ref, table_ref, extra_ref, out_ref, wide):
    base = pl.program_id(0) * per_step

    def one(s, state):
        buffer = wide.at[s % 2]
        for i in range(CAP):
            index = request_ref[base + s, half * PAD + i]
            buffer[pl.ds(i, 1), :] = table_ref[pl.ds(index, 1), :]
        buffer[CAP:, :] = extra_ref[s]
        out_ref[s] = buffer[...].astype(jnp.bfloat16)
        return state

    lax.fori_loop(0, per_step, one, 0)


def gather(half, requests, table, extra):
    devices = requests.shape[0]
    steps = 8
    per_step = devices // steps
    return pl.pallas_call(
        functools.partial(gather_kernel, half, per_step),
        grid=(steps,),
        in_specs=[
            pl.BlockSpec(memory_space=pltpu.SMEM),
            pl.BlockSpec(table.shape, lambda i: (0, 0)),
            pl.BlockSpec((per_step,) + extra.shape[1:], lambda i: (i, 0, 0)),
        ],
        out_specs=pl.BlockSpec((per_step, PAD, LANES), lambda i: (i, 0, 0)),
        out_shape=jax.ShapeDtypeStruct((devices, PAD, LANES), jnp.bfloat16),
        scratch_shapes=[pltpu.VMEM((2, PAD, LANES), jnp.float32)],
        compiler_params=pltpu.CompilerParams(vmem_limit_bytes=32 << 20),
        name="gather_rows",
    )(requests, table, extra)


def solve_kernel(
    blocks,
    gram_scale,
    slot_ref,
    count_ref,
    reply_ref,
    conf_ref,
    rating_ref,
    warm_ref,
    gram_ref,
    out_ref,
    wide,
    weight_wide,
    rows,
    turned,
    weighted,
    inside,
    x_ref,
    r_ref,
    p_ref,
    g_ref,
):
    sub = lax.broadcasted_iota(jnp.int32, (8, LANES), 0)
    lane = lax.broadcasted_iota(jnp.int32, (8, LANES), 1)
    top = sub < 4

    def fold(value):
        return value + pltpu.roll(value, 4, 0)

    def split(value):
        head = value.astype(jnp.bfloat16).astype(jnp.float32)
        return jnp.where(top, head, value - head).astype(jnp.bfloat16)

    def widen(i, state):
        start = pl.multiple_of(i * 512, 512)
        wide[pl.ds(start, 512), :] = reply_ref[pl.ds(start, 512), :].astype(jnp.float32)
        return state

    lax.fori_loop(0, reply_ref.shape[0] // 512, widen, 0)
    conf_turned = jnp.concatenate(
        [conf_ref[...], jnp.zeros((LANES - blocks, LANES), jnp.float32)], 0
    ).T
    for b in range(blocks):
        weight_wide[b] = jnp.broadcast_to(conf_turned[:, b : b + 1], (LANES, LANES))
    rows[...] = jnp.zeros_like(rows)

    def build(b, state):
        buffer = rows.at[b % 2]
        for t in range(LIVE):
            buffer[pl.ds(t, 1), :] = wide[pl.ds(slot_ref[b, t], 1), :]
        fetched = buffer[...]
        turned[b] = fetched.T.astype(jnp.bfloat16)
        weighted[b] = (weight_wide[b] * fetched).astype(jnp.bfloat16)
        end0 = count_ref[b, 0]
        end1 = end0 + count_ref[b, 1]
        end2 = end1 + count_ref[b, 2]
        end3 = end2 + count_ref[b, 3]
        which = sub % 4
        begin = jnp.where(which == 0, 0, jnp.where(which == 1, end0, jnp.where(which == 2, end1, end2)))
        end = jnp.where(which == 0, end0, jnp.where(which == 1, end1, jnp.where(which == 2, end2, end3)))
        mask = jnp.where((lane >= begin) & (lane < end), 1.0, 0.0)
        inside[b] = mask
        target = conf_ref[pl.ds(b, 1), :] * rating_ref[pl.ds(b, 1), :] * mask
        right = jnp.dot(
            split(target), fetched.astype(jnp.bfloat16), preferred_element_type=jnp.float32
        )
        r_ref[b] = fold(right)
        start = warm_ref[b]
        x_ref[b] = start
        p_ref[b] = start
        return state

    lax.fori_loop(0, blocks, build, 0)

    gram = gram_ref[...] * gram_scale
    gram_head = gram.astype(jnp.bfloat16)
    gram_tail = (gram - gram_head.astype(jnp.float32)).astype(jnp.bfloat16)
    gram_both = jnp.concatenate([gram_head, gram_tail], 1)
    group = 16

    def apply_system(g):
        ids = [g * group + c for c in range(group)]
        dirs = [p_ref[b] for b in ids]
        cut = [split(d) for d in dirs]
        shared = jnp.dot(jnp.concatenate(cut, 0), gram_both, preferred_element_type=jnp.float32)
        along = [
            fold(jnp.dot(cut[c], turned[ids[c]], preferred_element_type=jnp.float32))
            for c in range(group)
        ]
        back = [
            jnp.dot(
                split(along[c] * inside[ids[c]]),
                weighted[ids[c]],
                preferred_element_type=jnp.float32,
            )
            for c in range(group)
        ]
        images = []
        for c in range(group):
            part = shared[8 * c : 8 * c + 8]
            images.append(
                fold(back[c] + part[:, :LANES] + part[:, LANES:]) + ridge_weight * dirs[c]
            )
        return ids, dirs, images

    for g in range(blocks // group):
        ids, dirs, images = apply_system(g)
        for c in range(group):
            resid = r_ref[ids[c]] - images[c]
            r_ref[ids[c]] = resid
            p_ref[ids[c]] = resid
            g_ref[ids[c]] = jnp.broadcast_to(
                jnp.sum(resid * resid, -1, keepdims=True), (8, LANES)
            )

    def iterate(i, state):
        for g in range(blocks // group):
            ids, dirs, images = apply_system(g)
            for c in range(group):
                b = ids[c]
                norm_now = g_ref[b]
                step_size = norm_now / (
                    jnp.sum(dirs[c] * images[c], -1, keepdims=True) + guard_eps
                )
                x_ref[b] = x_ref[b] + step_size * dirs[c]
                resid = r_ref[b] - step_size * images[c]
                r_ref[b] = resid
                norm_next = jnp.sum(resid * resid, -1, keepdims=True)
                p_ref[b] = resid + norm_next / (norm_now + guard_eps) * dirs[c]
                g_ref[b] = jnp.broadcast_to(norm_next, (8, LANES))
        return state

    lax.fori_loop(0, ITERS, iterate, 0)
    out_ref[...] = x_ref[...]


def solve(slots, counts, replies, confidence, rating, warm_start, gram, gram_scale):
    blocks = counts.shape[0]
    doubled = jnp.concatenate([warm_start.reshape(blocks, 4, LANES)] * 2, 1)
    vmem = pl.BlockSpec(memory_space=pltpu.VMEM)
    smem = pl.BlockSpec(memory_space=pltpu.SMEM)
    state = pltpu.VMEM((blocks, 8, LANES), jnp.float32)
    solved = pl.pallas_call(
        functools.partial(solve_kernel, blocks, gram_scale),
        in_specs=[smem, smem, vmem, vmem, vmem, vmem, vmem],
        out_specs=vmem,
        out_shape=jax.ShapeDtypeStruct((blocks, 8, LANES), jnp.float32),
        scratch_shapes=[
            pltpu.VMEM(replies.shape, jnp.float32),
            pltpu.VMEM((blocks, LANES, LANES), jnp.float32),
            pltpu.VMEM((2, LANES, LANES), jnp.float32),
            pltpu.VMEM((blocks, LANES, LANES), jnp.bfloat16),
            pltpu.VMEM((blocks, LANES, LANES), jnp.bfloat16),
            state,
            state,
            state,
            state,
            state,
        ],
        compiler_params=pltpu.CompilerParams(vmem_limit_bytes=48 << 20),
        name="solve_rows",
    )(slots, counts, replies, confidence, rating, doubled, gram)
    return solved[:, :4].reshape(blocks * 4, LANES)


def exchange(values):
    return lax.all_to_all(values, AXES, split_axis=0, concat_axis=0, tiled=True)


def local_gram(table):
    return jnp.dot(
        table.T, table, precision=lax.Precision.HIGH, preferred_element_type=jnp.float32
    )


def three_parts(values):
    head = values.astype(jnp.bfloat16).astype(jnp.float32)
    rest = values - head
    middle = rest.astype(jnp.bfloat16).astype(jnp.float32)
    return head, middle, rest - middle


def shards(
    user_table,
    item_table,
    item_owner,
    item_row,
    user_confidence,
    user_rating,
    user_counts,
    user_owner,
    user_row,
    item_confidence,
    item_rating,
    item_counts,
):
    devices = lax.axis_size(AXES)
    tab_rows, width = user_table.shape
    blocks = user_counts.shape[0]
    batch = blocks * user_counts.shape[1]
    gram_scale = global_weight / (tab_rows * devices)

    def by_block(values):
        return values.reshape(blocks, -1)

    requests, slots = bucket(
        jnp.concatenate([by_block(item_owner), by_block(user_owner)], 0),
        jnp.concatenate([by_block(item_row), by_block(user_row)], 0),
    )
    item_gram = local_gram(item_table)
    came = exchange(jnp.concatenate([requests, item_gram], 1)[:, None, :])[:, 0]
    wanted = came[:, :width].astype(jnp.int32)
    gram_row = jnp.sum(came[:, width:], 0)
    extra = jnp.stack(three_parts(gram_row) + (jnp.zeros_like(gram_row),), 0)
    replies = exchange(
        gather(0, wanted, item_table, jnp.broadcast_to(extra[None], (devices, 4, width)))
    )
    item_gram = jnp.sum(replies[:, CAP:].astype(jnp.float32), 1)
    renewed = solve(
        slots[:blocks],
        user_counts,
        replies.reshape(-1, width),
        by_block(user_confidence),
        by_block(user_rating),
        user_table[:batch],
        item_gram,
        gram_scale,
    )
    new_users = jnp.concatenate([renewed, user_table[batch:]], 0)

    user_gram = local_gram(new_users)
    extra = jnp.stack(three_parts(user_gram) + (jnp.zeros_like(user_gram),), 1)
    replies = exchange(gather(1, wanted, new_users, extra))
    gram_row = jnp.sum(replies[:, CAP:].astype(jnp.float32), (0, 1))
    user_gram = exchange(jnp.broadcast_to(gram_row[None, None], (devices, 1, width)))[:, 0]
    renewed = solve(
        slots[blocks:],
        item_counts,
        replies.reshape(-1, width),
        by_block(item_confidence),
        by_block(item_rating),
        item_table[:batch],
        user_gram,
        gram_scale,
    )
    new_items = jnp.concatenate([renewed, item_table[batch:]], 0)
    return (new_users, new_items)


def solution(mesh):
    spec = P(AXES, None)
    flat = P(AXES)
    in_specs = (spec, spec, spec, flat, flat, flat, spec, spec, flat, flat, flat, spec)
    return jax.shard_map(
        shards, mesh=mesh, in_specs=in_specs, out_specs=(spec, spec), check_vma=False
    )
```

time: 1090 us -> 199 us (0.18)
  matrix products: 376 us -> 5.98 us
  local copies, waits for them, and re-layouts: 331 us -> 5.91 us
  waiting for transfers between devices: 291 us -> 78.4 us
  Pallas kernels: 0 us -> 76.9 us
  other arithmetic: 32 us -> 4.39 us
  between operations: 15.1 us -> 1 us
  starting transfers between devices: 37.4 us -> 26.2 us
    dot_general x24 -> x2, matrix products: 376 us -> 5.98 us  [local_gram(): jnp.dot(table.T, table, precision=lax.Precision.HIGH, preferred_element_t...]
    psum x2 -> x0, waiting for transfers between devices: 291 us -> none  [half_step(): global_gram = lax.psum(local_gram, ('gx', 'gy'))]
    gather x10 -> x0, local copies, waits for them, and re-layouts: 227 us -> none  [the longest x2 73.6 us: fetch_rows(): owner_starts[sorted_owner]]
    scatter x4 -> x0, local copies, waits for them, and re-layouts: 92.4 us -> none  [the longest x2 46.4 us: fetch_rows(): jnp.zeros((devices * capacity,), jnp.int32).at[send_slot].set(rows_local)]
    all_to_all x4, waiting for transfers between devices: 0.01 us -> 78.4 us  [exchange(): return lax.all_to_all(values, AXES, split_axis=0, concat_axis=0, tiled=True)]
    pallas_call x0 -> x5, Pallas kernels: none -> 76.9 us  [the longest x2 49.9 us: solve(): pl.pallas_call(functools.partial(solve_kernel, blocks, gram_scale), in_sp...]
    sort x2 -> x0, other arithmetic: 14.2 us -> none  [fetch_rows(): sorted_order = jnp.argsort(owner, stable=True)]
    all_to_all x4, starting transfers between devices: 37.3 us -> 26.2 us  [exchange(): return lax.all_to_all(values, AXES, split_axis=0, concat_axis=0, tiled=True)]
  transfers between devices with their start and end apart: 6 -> 4, of which waited for: 2 -> 4; matrix products, arithmetic and copies ran while one was open for 15% -> 0% of each run, Pallas kernels for 0% -> 0%
where the time goes in v1:
time: 199 us
  waiting for transfers between devices  78.4 us (39%)
  Pallas kernels  76.9 us (39%)
  starting transfers between devices  26.2 us (13%)
  matrix products  5.98 us (3%)
  local copies, waits for them, and re-layouts  5.91 us (3%)
  other arithmetic  4.39 us (2%)
    all_to_all x4, waiting for transfers between devices, exchange(): return lax.all_to_all(values, AXES, split_axis=0, concat_axis=0, tiled=True)  78.4 us
    pallas_call x2, Pallas kernels, solve(): pl.pallas_call(functools.partial(solve_kernel, blocks, gram_scale), in_sp...  49.9 us
    all_to_all x4, starting transfers between devices, exchange(): return lax.all_to_all(values, AXES, split_axis=0, concat_axis=0, tiled=True)  26.2 us
    pallas_call x2, Pallas kernels, gather(): pl.pallas_call(functools.partial(gather_kernel, half, per_step), grid=(st...  19.8 us
    pallas_call x1, Pallas kernels, bucket(): pl.pallas_call(functools.partial(bucket_kernel, chunks), out_shape=(jax.S...  7.25 us
    dot_general x2, matrix products, local_gram(): jnp.dot(table.T, table, precision=lax.Precision.HIGH, preferred_element_t...  5.98 us
    unnamed x31, local copies, waits for them, and re-layouts  4.15 us
  transfers between devices with their start and end apart: 4, of which 4 were waited for; matrix products, arithmetic and copies ran while one was open for 0% of the time, Pallas kernels for 0%

profile of v1, /device:TPU:1, one launch (start us, length us, event | category | flops | bytes accessed | tf_op | source)
XLA Modules:
  0.0 198.8 jit_solution(17941039053525139024)
XLA Ops:
  0.6 0.0 copy-start
  0.6 0.0 copy-start.9
  0.7 4.2 %fusion.5 = f32[128,128]{1,0:T(8,128)S(1)} fusion(f32[4096,128]{1,0:T(8,128)} %table_ref.1), kind=kOutput, calls=%fused_computation.24 | convolution fusion | flops 402653184 | bytes 2162688 | tf_op jit(solution)/shard_map/dot_general | solution.py:293
  4.9 7.3 %bucket.1 = (f32[128,128]{1,0:T(8,128)S(1)}, s32[96,128]{1,0:T(8,128)S(1)}) custom-call(s32[96,128]{1,0:T(8,128)S(1)} %get-tuple-element.15.owner_ref, s32[96,128]{1,0:T(8,128)S(1)} %get-tuple-element.16.row_ref), custom_call_target="tpu_custom_call" | custom-call | tf_op jit(solution)/shard_map/bucket/pallas_call | solution.py:77
  12.2 0.8 copy.20
  13.0 11.5 %all-to-all-start = ((f32[128,1,256]{2,1,0:T(1,128)}), f32[128,1,256]{2,1,0:T(1,128)S(1)}, u32[]{:S(2)}, u32[]{:S(2)}) async-start(f32[128,1,256]{2,1,0:T(1,128)} %copy.20), calls=%async_computation | async-start | bytes 262144 | tf_op jit(solution)/shard_map/all_to_all | solution.py:289
  24.5 0.1 pad.15.clone
  24.6 10.0 %all-to-all-done = f32[128,1,256]{2,1,0:T(1,128)S(1)} async-done(((f32[128,1,256]{2,1,0:T(1,128)}), f32[128,1,256]{2,1,0:T(1,128)S(1)}, u32[]{:S(2)}, u32[]{:S(2)}) %all-to-all-start) | async-done | bytes 131104 | tf_op jit(solution)/shard_map/all_to_all | solution.py:289
  34.6 0.1 maximum_maximum_fusion.1
  34.7 0.0 copy-done
  34.7 9.8 %gather_rows.2 = bf16[128,64,128]{2,1,0:T(8,128)(2,1)S(1)} custom-call(s32[128,128]{1,0:T(8,128)S(1)} %get-tuple-element.7.request_ref, f32[4096,128]{1,0:T(8,128)S(1)} %copy-done, f32[128,4,128]{2,1,0:T(4,128)S(1)} %broadcast_in_dim.7.extra_ref), custom_call_target="tpu_custom_call" | custom-call | tf_op jit(solution)/shard_map/gather_rows/pallas_call | solution.py:107
  44.5 0.0 copy-start.2
  44.5 1.3 copy-done.2
  45.8 5.0 %all-to-all-start.1 = ((bf16[128,64,128]{2,1,0:T(8,128)(2,1)}), bf16[128,64,128]{2,1,0:T(8,128)(2,1)}, u32[]{:S(2)}, u32[]{:S(2)}) async-start(bf16[128,64,128]{2,1,0:T(8,128)(2,1)} %copy-done.2), calls=%async_computation.1 | async-start | bytes 4194304 | tf_op jit(solution)/shard_map/all_to_all | solution.py:289
  50.8 0.0 copy-start.12
  50.8 0.0 slice-start.2
  50.8 0.0 copy-start.4
  50.8 0.0 copy-start.5
  50.8 0.6 copy-done.12
  51.5 0.1 copy.21.count_ref
  51.6 0.1 slice-done.2
  51.7 29.3 %all-to-all-done.1 = bf16[128,64,128]{2,1,0:T(8,128)(2,1)} async-done(((bf16[128,64,128]{2,1,0:T(8,128)(2,1)}), bf16[128,64,128]{2,1,0:T(8,128)(2,1)}, u32[]{:S(2)}, u32[]{:S(2)}) %all-to-all-start.1) | async-done | bytes 2097184 | tf_op jit(solution)/shard_map/all_to_all | solution.py:289
  81.1 1.3 convert_reduce_fusion.1.gram_ref
  82.4 24.9 %solve_rows.2 = f32[48,8,128]{2,1,0:T(8,128)S(1)} custom-call(s32[48,128]{1,0:T(8,128)S(1)} %get-tuple-element.12.slot_ref, s32[48,4]{1,0:T(8,128)S(1)} %copy.21.count_ref, bf16[8192,128]{1,0:T(8,128)(2,1)} %bitcast.6.reply_ref, f32[48,128]{1,0:T(8,128)S(1)} %bitcast.48, f32[48,128]{1,0:T(8,128)S(1)} %bitcast.49, ...), custom_call_target="tpu_custom_call" | custom-call | tf_op jit(solution)/shard_map/solve_rows/pallas_call | solution.py:265
  107.4 0.1 pad_maximum_fusion.table_ref
  107.5 0.0 copy-start.1
  107.5 1.8 convert_convert_fusion.1
  109.3 0.2 maximum_maximum_fusion.extra_ref
  109.5 0.0 copy-done.1
  109.6 10.0 %gather_rows.3 = bf16[128,64,128]{2,1,0:T(8,128)(2,1)S(1)} custom-call(s32[128,128]{1,0:T(8,128)S(1)} %get-tuple-element.7.request_ref, f32[4096,128]{1,0:T(8,128)S(1)} %pad_maximum_fusion.table_ref, f32[128,4,128]{2,1,0:T(4,128)S(1)} %maximum_maximum_fusion.extra_ref), custom_call_target="tpu_custom_call" | custom-call | tf_op jit(solution)/shard_map/gather_rows/pallas_call | solution.py:107
  119.6 0.0 copy-start.3
  119.6 1.3 copy-done.3
  120.9 5.4 %all-to-all-start.2 = ((bf16[128,64,128]{2,1,0:T(8,128)(2,1)}), bf16[128,64,128]{2,1,0:T(8,128)(2,1)}, u32[]{:S(2)}, u32[]{:S(2)}) async-start(bf16[128,64,128]{2,1,0:T(8,128)(2,1)} %copy-done.3), calls=%async_computation.2 | async-start | bytes 4194304 | tf_op jit(solution)/shard_map/all_to_all | solution.py:289
  126.3 0.0 copy-start.13
  126.3 0.0 slice-start
  126.4 0.0 copy-start.6
  126.4 0.0 copy-start.7
  126.4 0.6 copy-done.13
  127.0 0.1 copy.24.count_ref
  127.1 29.5 %all-to-all-done.2 = bf16[128,64,128]{2,1,0:T(8,128)(2,1)} async-done(((bf16[128,64,128]{2,1,0:T(8,128)(2,1)}), bf16[128,64,128]{2,1,0:T(8,128)(2,1)}, u32[]{:S(2)}, u32[]{:S(2)}) %all-to-all-start.2) | async-done | bytes 2097184 | tf_op jit(solution)/shard_map/all_to_all | solution.py:289
  156.6 1.1 convert_reduce_fusion
  157.7 0.7 broadcast_in_dim.8
  158.4 4.3 %all-to-all-start.3 = ((f32[128,1,128]{2,1,0:T(1,128)}), f32[128,1,128]{2,1,0:T(1,128)S(1)}, u32[]{:S(2)}, u32[]{:S(2)}) async-start(f32[128,1,128]{2,1,0:T(1,128)} %broadcast_in_dim.8), calls=%async_computation.3 | async-start | bytes 131072 | tf_op jit(solution)/shard_map/all_to_all | solution.py:289
  162.7 0.0 slice-done
  162.8 9.6 %all-to-all-done.3 = f32[128,1,128]{2,1,0:T(1,128)S(1)} async-done(((f32[128,1,128]{2,1,0:T(1,128)}), f32[128,1,128]{2,1,0:T(1,128)S(1)}, u32[]{:S(2)}, u32[]{:S(2)}) %all-to-all-start.3) | async-done | bytes 65568 | tf_op jit(solution)/shard_map/all_to_all | solution.py:289
  172.4 24.9 %solve_rows.3 = f32[48,8,128]{2,1,0:T(8,128)S(1)} custom-call(s32[48,128]{1,0:T(8,128)S(1)} %get-tuple-element.11.slot_ref, s32[48,4]{1,0:T(8,128)S(1)} %copy.24.count_ref, bf16[8192,128]{1,0:T(8,128)(2,1)} %bitcast.16.reply_ref, f32[48,128]{1,0:T(8,128)S(1)} %bitcast.50, f32[48,128]{1,0:T(8,128)S(1)} %bitcast.51, ...), custom_call_target="tpu_custom_call" | custom-call | tf_op jit(solution)/shard_map/solve_rows/pallas_call | solution.py:265
  197.4 0.0 slice-done.1
  197.4 1.5 pad_maximum_fusion.1
  (26 shorter events, 0.2 us)
Async XLA Ops:
  0.6 34.1 %copy-start = (f32[4096,128]{1,0:T(8,128)S(1)}, f32[4096,128]{1,0:T(8,128)}, u32[]{:S(2)}) copy-start(f32[4096,128]{1,0:T(8,128)} %table_ref.1) | copy-start | bytes 6291460
  0.6 4.2 %copy-start.9 = (s32[6144,1]{0,1:T(1,128)S(1)}, s32[6144,1]{0,1:T(1,128)}, u32[]{:S(2)}) copy-start(s32[6144,1]{0,1:T(1,128)} %param.14) | copy-start | bytes 73732
  0.7 4.2 %copy-start.8 = (s32[6144,1]{0,1:T(1,128)S(1)}, s32[6144,1]{0,1:T(1,128)}, u32[]{:S(2)}) copy-start(s32[6144,1]{0,1:T(1,128)} %param.19) | copy-start | bytes 73732
  0.7 4.2 %copy-start.11 = (s32[6144]{0:T(1024)S(1)}, s32[6144]{0:T(1024)}, u32[]{:S(2)}) copy-start(s32[6144]{0:T(1024)} %param.15) | copy-start | bytes 73732
  0.7 4.2 %copy-start.10 = (s32[6144]{0:T(1024)S(1)}, s32[6144]{0:T(1024)}, u32[]{:S(2)}) copy-start(s32[6144]{0:T(1024)} %param.20) | copy-start | bytes 73732
  13.0 21.5 %all-to-all-start = ((f32[128,1,256]{2,1,0:T(1,128)}), f32[128,1,256]{2,1,0:T(1,128)S(1)}, u32[]{:S(2)}, u32[]{:S(2)}) async-start(f32[128,1,256]{2,1,0:T(1,128)} %copy.20), calls=%async_computation | async-start | bytes 262144 | tf_op jit(solution)/shard_map/all_to_all | solution.py:289
  44.5 1.3 copy-start.2
  45.8 35.3 %all-to-all-start.1 = ((bf16[128,64,128]{2,1,0:T(8,128)(2,1)}), bf16[128,64,128]{2,1,0:T(8,128)(2,1)}, u32[]{:S(2)}, u32[]{:S(2)}) async-start(bf16[128,64,128]{2,1,0:T(8,128)(2,1)} %copy-done.2), calls=%async_computation.1 | async-start | bytes 4194304 | tf_op jit(solution)/shard_map/all_to_all | solution.py:289
  50.8 0.7 copy-start.12
  50.8 0.9 slice-start.2
  50.8 31.6 %copy-start.4 = (f32[6144]{0:T(1024)S(1)}, f32[6144]{0:T(1024)}, u32[]{:S(2)}) copy-start(f32[6144]{0:T(1024)} %param.16) | copy-start | bytes 73732
  50.8 31.6 %copy-start.5 = (f32[6144]{0:T(1024)S(1)}, f32[6144]{0:T(1024)}, u32[]{:S(2)}) copy-start(f32[6144]{0:T(1024)} %param.17) | copy-start | bytes 73732
  81.1 26.3 %slice-start.3 = ((f32[4096,128]{1,0:T(8,128)}), f32[3904,128]{1,0:T(8,128)S(1)}, s32[]{:S(2)}) async-start(f32[4096,128]{1,0:T(8,128)} %param.12), calls=%async_computation.7 | async-start | bytes 3997696 | tf_op jit(solution)/shard_map/slice | solution.py:351
  107.5 2.0 %copy-start.1 = (f32[4096,128]{1,0:T(8,128)}, f32[4096,128]{1,0:T(8,128)S(1)}, u32[]{:S(2)}) copy-start(f32[4096,128]{1,0:T(8,128)S(1)} %pad_maximum_fusion.table_ref) | copy-start | bytes 6291460
  119.6 1.3 copy-start.3
  120.9 35.8 %all-to-all-start.2 = ((bf16[128,64,128]{2,1,0:T(8,128)(2,1)}), bf16[128,64,128]{2,1,0:T(8,128)(2,1)}, u32[]{:S(2)}, u32[]{:S(2)}) async-start(bf16[128,64,128]{2,1,0:T(8,128)(2,1)} %copy-done.3), calls=%async_computation.2 | async-start | bytes 4194304 | tf_op jit(solution)/shard_map/all_to_all | solution.py:289
  126.3 0.7 copy-start.13
  126.3 36.4 %slice-start = ((f32[4096,128]{1,0:T(8,128)}), f32[192,128]{1,0:T(8,128)S(1)}, s32[]{:S(2)}) async-start(f32[4096,128]{1,0:T(8,128)} %table_ref.1), calls=%async_computation.4 | async-start | bytes 196608 | tf_op jit(solution)/shard_map/slice | solution.py:364
  126.4 46.1 %copy-start.6 = (f32[6144]{0:T(1024)S(1)}, f32[6144]{0:T(1024)}, u32[]{:S(2)}) copy-start(f32[6144]{0:T(1024)} %param.21) | copy-start | bytes 73732
  126.4 46.0 %copy-start.7 = (f32[6144]{0:T(1024)S(1)}, f32[6144]{0:T(1024)}, u32[]{:S(2)}) copy-start(f32[6144]{0:T(1024)} %param.22) | copy-start | bytes 73732
  127.0 70.4 %slice-start.1 = ((f32[4096,128]{1,0:T(8,128)}), f32[3904,128]{1,0:T(8,128)S(1)}, s32[]{:S(2)}) async-start(f32[4096,128]{1,0:T(8,128)} %table_ref.1), calls=%async_computation.5 | async-start | bytes 3997696 | tf_op jit(solution)/shard_map/slice | solution.py:368
  158.4 14.0 %all-to-all-start.3 = ((f32[128,1,128]{2,1,0:T(1,128)}), f32[128,1,128]{2,1,0:T(1,128)S(1)}, u32[]{:S(2)}, u32[]{:S(2)}) async-start(f32[128,1,128]{2,1,0:T(1,128)} %broadcast_in_dim.8), calls=%async_computation.3 | async-start | bytes 131072 | tf_op jit(solution)/shard_map/all_to_all | solution.py:289

commit v2 on v1

v2 whole, which is shorter than its diff:
```python
import functools

import jax
import jax.numpy as jnp
from jax import lax
from jax.experimental import pallas as pl
from jax.experimental.pallas import tpu as pltpu
from jax.sharding import PartitionSpec as P

ITERS = 8
AXES = ("gx", "gy")
LIVE = 112
PAD = 64
CAP = 60
PATCH = 14
SLOT = 16
EARLY = 48
EAGER = 6
TOGETHER = 4
LANES = 128

ridge_weight = 1.0
global_weight = 256.0
guard_eps = 1e-06


def bucket_kernel(batch, owner0, row0, owner1, row1, gram_ref, request_ref, slot0, slot1, place_ref):
    chunks = owner0.shape[0]
    sub = lax.broadcasted_iota(jnp.int32, (LANES, LANES), 0)
    lane = lax.broadcasted_iota(jnp.int32, (LANES, LANES), 1)
    below = jnp.where(sub < lane, 1.0, 0.0)
    prefix = jnp.concatenate([below, jnp.ones_like(below)], 1).astype(jnp.bfloat16)
    place = sub % PAD
    first_half = sub < PAD
    group = 8
    zero = jnp.zeros((LANES, LANES), jnp.float32)

    def step(half, g, state):
        carry, wanted = state
        start = pl.multiple_of(g * group, group)
        owners = (owner0, owner1)[half][pl.ds(start, group), :]
        rows = (row0, row1)[half][pl.ds(start, group), :]
        position = lax.broadcasted_iota(jnp.int32, owners.shape, 1)
        masked = jnp.where(position < LIVE, owners, -1)
        unit = jnp.where(rows < batch, 1.0, float(PAD)) if half == 1 else None
        hot = []
        counted = []
        for c in range(group):
            hit = sub == masked[c : c + 1, :]
            hot.append(jnp.where(hit, 1.0, 0.0))
            tally = hot[c] if half == 0 else jnp.where(hit, unit[c : c + 1, :], 0.0)
            counted.append(
                jnp.dot(tally.astype(jnp.bfloat16), prefix, preferred_element_type=jnp.float32)
            )
        ranks = []
        for c in range(group):
            before = counted[c][:, :LANES] + carry
            ranks.append(jnp.sum(before * hot[c], 0, keepdims=True).astype(jnp.int32))
            carry = carry + counted[c][:, LANES:]
        ranks = jnp.concatenate(ranks, 0)
        if half == 1:
            ranks = jnp.where(rows < batch, ranks % PAD, CAP - 1 - ranks // PAD)
        high = (rows // PAD).astype(jnp.float32)
        low = (rows % PAD).astype(jnp.float32)
        if half == 1:
            high, low = low, high
        lane_row = position.astype(jnp.float32)
        for c in range(group):
            chosen = place == ranks[c : c + 1, :]
            value = jnp.where(first_half, high[c : c + 1, :], low[c : c + 1, :])
            put = jnp.where(chosen, value, 0.0).astype(jnp.bfloat16)
            if half == 1:
                spot = jnp.where(
                    first_half, lane_row[c : c + 1, :], (g * group + c).astype(jnp.float32)
                )
                put = jnp.concatenate(
                    [put, jnp.where(chosen, spot, 0.0).astype(jnp.bfloat16)], 0
                )
            wanted = wanted + lax.dot_general(
                hot[c].astype(jnp.bfloat16),
                put,
                (((1,), (1,)), ((), ())),
                preferred_element_type=jnp.float32,
            )
        if half == 0:
            slot0[pl.ds(start, group), :] = owners * PAD + ranks
        else:
            slot1[pl.ds(start, group), :] = owners * EARLY + jnp.where(
                ranks < PATCH, EARLY - 1, ranks - PATCH
            )
        return carry, wanted

    steps = chunks // group
    _, first = lax.fori_loop(0, steps, functools.partial(step, 0), (zero, zero))
    wide = jnp.concatenate([zero, zero], 1)
    tally, second = lax.fori_loop(0, steps, functools.partial(step, 1), (zero, wide))
    spots = second[:, LANES:]
    second = second[:, :LANES]
    first = first * PAD + pltpu.roll(first, PAD, 1)
    second = second * PAD + pltpu.roll(second, PAD, 1)
    spots = spots + pltpu.roll(spots, PAD, 1) * LANES
    renewed = tally.astype(jnp.int32) % PAD
    most = jnp.max(renewed).astype(jnp.float32)
    request = jnp.where(lane < PAD, first, second)
    request_ref[:, :LANES] = jnp.where(lane == LANES - 1, most, request)
    request_ref[:, LANES:] = gram_ref[...]
    others = tally.astype(jnp.int32) // PAD
    used = (lane < renewed) | (lane >= CAP - others)
    places = jnp.where(used, spots.astype(jnp.int32), chunks * LANES)
    looked = jnp.where(others > CAP - PATCH, PATCH, jnp.minimum(renewed, PATCH))
    places = jnp.where(lane == PAD - 2, looked, places)
    place_ref[...] = jnp.where(lane == PAD - 1, renewed, places)


def bucket(owner0, row0, owner1, row1, gram, batch):
    slots = jax.ShapeDtypeStruct(owner0.shape, jnp.int32)
    return pl.pallas_call(
        functools.partial(bucket_kernel, batch),
        out_shape=(
            jax.ShapeDtypeStruct((LANES, 2 * LANES), jnp.float32),
            slots,
            slots,
            jax.ShapeDtypeStruct((LANES, LANES), jnp.int32),
        ),
        compiler_params=pltpu.CompilerParams(vmem_limit_bytes=32 << 20),
        name="bucket",
    )(owner0, row0, owner1, row1, gram)


def gather_kernel(first, count, per_step, request_ref, table_ref, *refs):
    out_ref, wide = refs[-2:]
    base = pl.program_id(0) * per_step
    depth = wide.shape[1]
    last = jnp.zeros((depth - count, LANES), jnp.float32)
    if len(refs) == 3:
        row = refs[0][...]
        head = row.astype(jnp.bfloat16).astype(jnp.float32)
        last = jnp.concatenate([head, row - head, last[2:]], 0)
    for k in range(2):
        wide[k, count:, :] = last

    def one(s, state):
        buffer = wide.at[s % 2]
        for i in range(count):
            index = request_ref[base + s, first + i]
            buffer[pl.ds(i, 1), :] = table_ref[pl.ds(index, 1), :]
        out_ref[s] = buffer[...].astype(jnp.bfloat16)
        return state

    lax.fori_loop(0, per_step, one, 0)


def gather(first, count, depth, requests, table, extra=None):
    devices = requests.shape[0]
    steps = 8
    per_step = devices // steps
    more = () if extra is None else (extra,)
    return pl.pallas_call(
        functools.partial(gather_kernel, first, count, per_step),
        grid=(steps,),
        in_specs=[
            pl.BlockSpec(memory_space=pltpu.SMEM),
            pl.BlockSpec(table.shape, lambda i: (0, 0)),
        ]
        + [pl.BlockSpec(extra.shape, lambda i: (0, 0)) for extra in more],
        out_specs=pl.BlockSpec((per_step, depth, LANES), lambda i: (i, 0, 0)),
        out_shape=pltpu.HBM((devices, depth, LANES), jnp.bfloat16),
        scratch_shapes=[pltpu.VMEM((2, depth, LANES), jnp.float32)],
        compiler_params=pltpu.CompilerParams(vmem_limit_bytes=32 << 20),
        name="gather_rows",
    )(requests, table, *more)


def unsort_kernel(slot_ref, reply_ref, out_ref, wide):
    widen(reply_ref, wide)

    def one(b, state):
        for t in range(LIVE):
            out_ref[b, pl.ds(t, 1), :] = wide[pl.ds(slot_ref[b, t], 1), :]
        out_ref[b, LIVE:, :] = jnp.zeros((LANES - LIVE, LANES), jnp.float32)
        return state

    lax.fori_loop(0, out_ref.shape[0], one, 0)


def unsort(slots, replies):
    blocks = slots.shape[0]
    return pl.pallas_call(
        unsort_kernel,
        in_specs=[pl.BlockSpec(memory_space=pltpu.SMEM), pl.BlockSpec(memory_space=pltpu.VMEM)],
        out_specs=pl.BlockSpec(memory_space=pltpu.VMEM),
        out_shape=pltpu.VMEM((blocks, LANES, LANES), jnp.float32),
        scratch_shapes=[pltpu.VMEM(replies.shape, jnp.float32)],
        compiler_params=pltpu.CompilerParams(vmem_limit_bytes=32 << 20),
        name="unsort_rows",
    )(slots, replies)


def fold(value):
    return value + pltpu.roll(value, 4, 0)


def split(value):
    top = lax.broadcasted_iota(jnp.int32, value.shape, 0) < 4
    head = value.astype(jnp.bfloat16).astype(jnp.float32)
    return jnp.where(top, head, value - head).astype(jnp.bfloat16)


def widen(source, target):
    step = 512

    def one(i, state):
        start = pl.multiple_of(i * step, step)
        target[pl.ds(start, step), :] = source[pl.ds(start, step), :].astype(jnp.float32)
        return state

    lax.fori_loop(0, source.shape[0] // step, one, 0)


def spread_weights(conf_ref, weight_wide):
    blocks = conf_ref.shape[0]
    conf_turned = jnp.concatenate(
        [conf_ref[...], jnp.zeros((LANES - blocks, LANES), jnp.float32)], 0
    ).T
    for b in range(blocks):
        weight_wide[b] = jnp.broadcast_to(conf_turned[:, b : b + 1], (LANES, LANES))


def build_blocks(
    first, rows, count_ref, conf_ref, rating_ref, weight_wide, turned, weighted, inside, right
):
    sub = lax.broadcasted_iota(jnp.int32, (8, LANES), 0)
    lane = lax.broadcasted_iota(jnp.int32, (8, LANES), 1)
    which = sub % 4
    sums = []
    for c, fetched in enumerate(rows):
        b = first + c
        turned[b] = fetched.T.astype(jnp.bfloat16)
        weighted[b] = (weight_wide[b] * fetched).astype(jnp.bfloat16)
        end0 = count_ref[b, 0]
        end1 = end0 + count_ref[b, 1]
        end2 = end1 + count_ref[b, 2]
        end3 = end2 + count_ref[b, 3]
        begin = jnp.where(which < 2, jnp.where(which == 0, 0, end0), jnp.where(which == 2, end1, end2))
        end = jnp.where(which < 2, jnp.where(which == 0, end0, end1), jnp.where(which == 2, end2, end3))
        mask = jnp.where((lane >= begin) & (lane < end), 1.0, 0.0)
        inside[b] = mask
        target = conf_ref[pl.ds(b, 1), :] * rating_ref[pl.ds(b, 1), :] * mask
        sums.append(
            jnp.dot(split(target), fetched.astype(jnp.bfloat16), preferred_element_type=jnp.float32)
        )
    for c, part in enumerate(sums):
        right[first + c] = fold(part)


def start_from(warm_ref, x_ref, p_ref):
    for b in range(x_ref.shape[0]):
        warm = warm_ref[pl.ds(4 * b, 4), :]
        both = jnp.concatenate([warm, warm], 0)
        x_ref[b] = both
        p_ref[b] = both


def give(x_ref, out_ref):
    for b in range(x_ref.shape[0]):
        out_ref[pl.ds(4 * b, 4), :] = x_ref[b, :4, :]


def conjugate(gram, turned, weighted, inside, x_ref, r_ref, p_ref, g_ref):
    blocks = x_ref.shape[0]
    gram_head = gram.astype(jnp.bfloat16)
    gram_tail = (gram - gram_head.astype(jnp.float32)).astype(jnp.bfloat16)
    gram_both = jnp.concatenate([gram_head, gram_tail], 1)
    group = 16

    def apply_system(g):
        ids = [g * group + c for c in range(group)]
        dirs = [p_ref[b] for b in ids]
        cut = [split(d) for d in dirs]
        shared = jnp.dot(jnp.concatenate(cut, 0), gram_both, preferred_element_type=jnp.float32)
        along = [
            fold(jnp.dot(cut[c], turned[ids[c]], preferred_element_type=jnp.float32))
            for c in range(group)
        ]
        back = [
            jnp.dot(
                split(along[c] * inside[ids[c]]),
                weighted[ids[c]],
                preferred_element_type=jnp.float32,
            )
            for c in range(group)
        ]
        images = []
        for c in range(group):
            part = shared[8 * c : 8 * c + 8]
            images.append(
                fold(back[c] + part[:, :LANES] + part[:, LANES:]) + ridge_weight * dirs[c]
            )
        return ids, dirs, images

    for g in range(blocks // group):
        ids, dirs, images = apply_system(g)
        for c in range(group):
            resid = r_ref[ids[c]] - images[c]
            r_ref[ids[c]] = resid
            p_ref[ids[c]] = resid
            g_ref[ids[c]] = jnp.broadcast_to(
                jnp.sum(resid * resid, -1, keepdims=True), (8, LANES)
            )

    def iterate(i, state):
        for g in range(blocks // group):
            ids, dirs, images = apply_system(g)
            for c in range(group):
                b = ids[c]
                norm_now = g_ref[b]
                step_size = norm_now / (
                    jnp.sum(dirs[c] * images[c], -1, keepdims=True) + guard_eps
                )
                x_ref[b] = x_ref[b] + step_size * dirs[c]
                resid = r_ref[b] - step_size * images[c]
                r_ref[b] = resid
                norm_next = jnp.sum(resid * resid, -1, keepdims=True)
                p_ref[b] = resid + norm_next / (norm_now + guard_eps) * dirs[c]
                g_ref[b] = jnp.broadcast_to(norm_next, (8, LANES))
        return state

    lax.fori_loop(0, ITERS, iterate, 0)


def solve_users_kernel(
    gram_scale,
    slot_ref,
    wanted_ref,
    count_ref,
    reply_ref,
    conf_ref,
    rating_ref,
    table_ref,
    still_ref,
    out_ref,
    patch_ref,
    wide,
    weight_wide,
    rows,
    turned,
    weighted,
    inside,
    x_ref,
    r_ref,
    p_ref,
    g_ref,
):
    blocks = conf_ref.shape[0]
    batch = 4 * blocks
    widen(reply_ref, wide)
    spread_weights(conf_ref, weight_wide)
    rows[...] = jnp.zeros_like(rows)

    def build(g, state):
        first = g * TOGETHER
        for c in range(TOGETHER):
            for t in range(LIVE):
                rows[c, pl.ds(t, 1), :] = wide[pl.ds(slot_ref[first + c, t], 1), :]
        build_blocks(
            first,
            [rows[c] for c in range(TOGETHER)],
            count_ref,
            conf_ref,
            rating_ref,
            weight_wide,
            turned,
            weighted,
            inside,
            r_ref,
        )
        return state

    lax.fori_loop(0, blocks // TOGETHER, build, 0)
    start_from(table_ref, x_ref, p_ref)
    gram = wide[pl.ds(CAP, LANES, stride=PAD), :] + wide[pl.ds(CAP + 1, LANES, stride=PAD), :]
    conjugate(gram * gram_scale, turned, weighted, inside, x_ref, r_ref, p_ref, g_ref)
    give(x_ref, out_ref)

    table = wide.at[pl.ds(0, table_ref.shape[0])]
    solved = out_ref[...]
    table[pl.ds(0, batch), :] = solved
    step = 64

    def copy(i, state):
        start = pl.multiple_of(batch + i * step, step)
        table[pl.ds(start, step), :] = table_ref[pl.ds(start, step), :]
        return state

    lax.fori_loop(0, (table_ref.shape[0] - batch) // step, copy, 0)
    head = solved.astype(jnp.bfloat16)
    rest = (solved - head.astype(jnp.float32)).astype(jnp.bfloat16)
    head_turned = head.astype(jnp.float32).T.astype(jnp.bfloat16)
    cross = jnp.dot(head_turned, rest, preferred_element_type=jnp.float32)
    gram = jnp.dot(head_turned, head, preferred_element_type=jnp.float32) + cross + cross.T
    rows[0] = still_ref[...] + gram

    def one(o, state):
        buffer = rows.at[1, pl.ds(pl.multiple_of(o % 2 * SLOT, SLOT), SLOT)]
        for i in range(PATCH):
            buffer[pl.ds(i, 1), :] = table[pl.ds(wanted_ref[o, PAD + i], 1), :]
        share = rows[0, pl.ds(o, 1), :]
        top = share.astype(jnp.bfloat16).astype(jnp.float32)
        buffer[pl.ds(PATCH, 1), :] = top
        buffer[pl.ds(PATCH + 1, 1), :] = share - top
        patch_ref[o] = buffer[...].astype(jnp.bfloat16)
        return state

    lax.fori_loop(0, wanted_ref.shape[0], one, 0)


def solve_users(slots, wanted, counts, replies, confidence, rating, table, still, gram_scale):
    blocks = confidence.shape[0]
    vmem = pl.BlockSpec(memory_space=pltpu.VMEM)
    smem = pl.BlockSpec(memory_space=pltpu.SMEM)
    state = pltpu.VMEM((blocks, 8, LANES), jnp.float32)
    matrices = pltpu.VMEM((blocks, LANES, LANES), jnp.bfloat16)
    return pl.pallas_call(
        functools.partial(solve_users_kernel, gram_scale),
        in_specs=[smem] * 3 + [vmem] * 5,
        out_specs=[vmem, vmem],
        out_shape=[
            jax.ShapeDtypeStruct((4 * blocks, LANES), jnp.float32),
            pltpu.HBM((wanted.shape[0], SLOT, LANES), jnp.bfloat16),
        ],
        scratch_shapes=[
            pltpu.VMEM(replies.shape, jnp.float32),
            pltpu.VMEM((blocks, LANES, LANES), jnp.float32),
            pltpu.VMEM((TOGETHER, LANES, LANES), jnp.float32),
            matrices,
            matrices,
        ]
        + [state] * 5,
        compiler_params=pltpu.CompilerParams(vmem_limit_bytes=48 << 20),
        name="solve_users",
    )(slots, wanted, counts, replies, confidence, rating, table, still)


def build_items_kernel(
    place_ref,
    count_ref,
    rows_ref,
    patch_ref,
    more_ref,
    conf_ref,
    rating_ref,
    turned,
    weighted,
    inside,
    right,
    wide,
    more_narrow,
    more_wide,
    weight_wide,
    rows,
):
    blocks = conf_ref.shape[0]
    widen(patch_ref, wide)
    spread_weights(conf_ref, weight_wide)

    def copy(b, state):
        rows[pl.ds(pl.multiple_of(b * LANES, LANES), LANES), :] = rows_ref[b]
        return state

    lax.fori_loop(0, blocks, copy, 0)

    def renew(o, state):
        def put(k):
            rows[pl.ds(place_ref[o, k], 1), :] = wide[pl.ds(o * SLOT + k, 1), :]

        for k in range(EAGER):
            put(k)

        @pl.when(place_ref[o, PAD - 2] > EAGER)
        def _():
            for k in range(EAGER, PATCH):
                put(k)

        count = place_ref[o, PAD - 1]

        @pl.when(count > PATCH)
        def _():
            pltpu.sync_copy(more_ref.at[o], more_narrow)
            more_wide[...] = more_narrow[...].astype(jnp.float32)

            def put_more(k, inner):
                rows[pl.ds(place_ref[o, k], 1), :] = more_wide[pl.ds(k - PATCH, 1), :]
                return inner

            lax.fori_loop(PATCH, count, put_more, 0)

        return state

    lax.fori_loop(0, place_ref.shape[0], renew, 0)

    def build(g, state):
        first = g * TOGETHER
        start = pl.multiple_of(first * LANES, LANES)
        build_blocks(
            first,
            [rows[pl.ds(start + c * LANES, LANES), :] for c in range(TOGETHER)],
            count_ref,
            conf_ref,
            rating_ref,
            weight_wide,
            turned,
            weighted,
            inside,
            right,
        )
        return state

    lax.fori_loop(0, blocks // TOGETHER, build, 0)


def build_items(places, counts, rows, patch, more, confidence, rating):
    blocks = confidence.shape[0]
    vmem = pl.BlockSpec(memory_space=pltpu.VMEM)
    smem = pl.BlockSpec(memory_space=pltpu.SMEM)
    matrices = pltpu.VMEM((blocks, LANES, LANES), jnp.bfloat16)
    vectors = pltpu.VMEM((blocks, 8, LANES), jnp.float32)
    return pl.pallas_call(
        build_items_kernel,
        in_specs=[smem] * 2 + [vmem] * 2 + [pl.BlockSpec(memory_space=pl.ANY)] + [vmem] * 2,
        out_specs=[vmem] * 4,
        out_shape=[matrices, matrices, vectors, vectors],
        scratch_shapes=[
            pltpu.VMEM(patch.shape, jnp.float32),
            pltpu.VMEM(more.shape[1:], jnp.bfloat16),
            pltpu.VMEM(more.shape[1:], jnp.float32),
            pltpu.VMEM((blocks, LANES, LANES), jnp.float32),
            pltpu.VMEM((blocks * LANES + 8, LANES), jnp.float32),
        ],
        compiler_params=pltpu.CompilerParams(vmem_limit_bytes=48 << 20),
        name="build_items",
    )(places, counts, rows, patch, more, confidence, rating)


def solve_items_kernel(
    gram_scale,
    turned,
    weighted,
    inside,
    right,
    warm_ref,
    gram_ref,
    table_ref,
    out_ref,
    x_ref,
    r_ref,
    p_ref,
    g_ref,
    solved,
    sems,
):
    batch = solved.shape[0]
    rest = pl.ds(batch, table_ref.shape[0] - batch)
    keep = pltpu.make_async_copy(table_ref.at[rest], out_ref.at[rest], sems.at[0])
    keep.start()
    start_from(warm_ref, x_ref, p_ref)
    r_ref[...] = right[...]
    conjugate(gram_ref[...] * gram_scale, turned, weighted, inside, x_ref, r_ref, p_ref, g_ref)
    give(x_ref, solved)
    put = pltpu.make_async_copy(solved, out_ref.at[pl.ds(0, batch)], sems.at[1])
    put.start()
    put.wait()
    keep.wait()


def solve_items(built, table, gram, gram_scale):
    blocks = built[0].shape[0]
    vmem = pl.BlockSpec(memory_space=pltpu.VMEM)
    hbm = pl.BlockSpec(memory_space=pltpu.HBM)
    return pl.pallas_call(
        functools.partial(solve_items_kernel, gram_scale),
        in_specs=[vmem] * 6 + [hbm],
        out_specs=hbm,
        out_shape=jax.ShapeDtypeStruct(table.shape, jnp.float32),
        scratch_shapes=[pltpu.VMEM((blocks, 8, LANES), jnp.float32)] * 4
        + [pltpu.VMEM((4 * blocks, LANES), jnp.float32), pltpu.SemaphoreType.DMA((2,))],
        compiler_params=pltpu.CompilerParams(vmem_limit_bytes=32 << 20),
        name="solve_items",
    )(*built, table[: 4 * blocks], gram, table)


def exchange(values):
    return lax.all_to_all(values, AXES, split_axis=0, concat_axis=0, tiled=True)


def local_gram(table):
    return jnp.dot(
        table.T, table, precision=lax.Precision.HIGH, preferred_element_type=jnp.float32
    )


def shards(
    user_table,
    item_table,
    item_owner,
    item_row,
    user_confidence,
    user_rating,
    user_counts,
    user_owner,
    user_row,
    item_confidence,
    item_rating,
    item_counts,
):
    devices = lax.axis_size(AXES)
    tab_rows, width = user_table.shape
    blocks = user_counts.shape[0]
    batch = blocks * user_counts.shape[1]
    gram_scale = global_weight / (tab_rows * devices)

    def by_block(values):
        return values.reshape(blocks, -1)

    requests, item_slots, user_slots, places = bucket(
        by_block(item_owner),
        by_block(item_row),
        by_block(user_owner),
        by_block(user_row),
        local_gram(item_table),
        batch,
    )
    came = exchange(requests[:, None, :])[:, 0]
    wanted = came[:, :width].astype(jnp.int32)
    gram_row = jnp.sum(came[:, width:], 0, keepdims=True)
    most = jnp.max(wanted[:, -1])
    fresh = jnp.minimum(wanted[:, PAD : 2 * PAD], batch - 1)

    replies = exchange(gather(0, CAP, PAD, wanted, item_table, gram_row))
    early = gather(PAD + PATCH, CAP - PATCH, EARLY, wanted, user_table)
    still = local_gram(user_table[batch:])
    early, still, replies = lax.optimization_barrier((early, still, replies))
    early = exchange(early)
    renewed, patch = solve_users(
        item_slots,
        wanted,
        user_counts,
        replies.reshape(-1, width),
        by_block(user_confidence),
        by_block(user_rating),
        user_table,
        still,
        gram_scale,
    )
    new_users = jnp.concatenate([renewed, user_table[batch:]], 0)

    patch, early = lax.optimization_barrier((patch, early))
    patch = exchange(patch)
    narrow = renewed.astype(jnp.bfloat16)

    def another(state):
        done, kept = state
        rows = narrow[lax.dynamic_slice_in_dim(fresh, done, SLOT, 1)]
        return done + SLOT, lax.dynamic_update_slice(kept, exchange(rows), (0, done - PATCH, 0))

    _, more = lax.while_loop(lambda state: state[0] < most, another, (jnp.int32(PATCH), replies))
    rows = unsort(user_slots, early.reshape(-1, width))
    patch, rows = lax.optimization_barrier((patch, rows))
    gram_row = jnp.sum(patch[:, PATCH:].astype(jnp.float32), (0, 1))
    user_gram = exchange(jnp.broadcast_to(gram_row[None, None], (devices, 1, width)))[:, 0]
    built = build_items(
        places,
        item_counts,
        rows,
        patch.reshape(-1, width),
        more,
        by_block(item_confidence),
        by_block(item_rating),
    )
    return (new_users, solve_items(built, item_table, user_gram, gram_scale))


def solution(mesh):
    spec = P(AXES, None)
    flat = P(AXES)
    in_specs = (spec, spec, spec, flat, flat, flat, spec, spec, flat, flat, flat, spec)
    return jax.shard_map(
        shards, mesh=mesh, in_specs=in_specs, out_specs=(spec, spec), check_vma=False
    )
```

time: 199 us -> 177 us (0.89)
  waiting for transfers between devices: 78.4 us -> 17.6 us
  blocking collectives: 0 us -> 21.4 us
  local copies, waits for them, and re-layouts: 5.91 us -> 13.9 us
  Pallas kernels: 76.9 us -> 80.4 us
  starting transfers between devices: 26.2 us -> 28.8 us
  matrix products: 5.98 us -> 8.1 us
    all_to_all x4, waiting for transfers between devices: 78.4 us -> 17.6 us  [exchange(): return lax.all_to_all(values, AXES, split_axis=0, concat_axis=0, tiled=True)]
    all_to_all x0 -> x1, blocking collectives: none -> 21.4 us  [exchange(): return lax.all_to_all(values, AXES, split_axis=0, concat_axis=0, tiled=True)]
    unnamed x31 -> x39, local copies, waits for them, and re-layouts: 4.15 us -> 10.2 us
    pallas_call x5 -> x7, Pallas kernels: 76.9 us -> 80.4 us  [the longest x1 25.7 us: solve_users(): pl.pallas_call(functools.partial(solve_users_kernel, gram_scale), in_spec...]
    concatenate x1, other arithmetic: 0.14 us -> 3.02 us  [shards(): new_users = jnp.concatenate([renewed, user_table[batch:]], 0)]
    slice x11 -> x2, local copies, waits for them, and re-layouts: 0.19 us -> 2.98 us  [the longest x1 2.97 us: shards(): still = local_gram(user_table[batch:])]
    all_to_all x4, starting transfers between devices: 26.2 us -> 28.8 us  [exchange(): return lax.all_to_all(values, AXES, split_axis=0, concat_axis=0, tiled=True)]
    reduce_sum x3 -> x2, other arithmetic: 2.43 us -> 0.18 us  [the longest x1 0.15 us: shards(): gram_row = jnp.sum(patch[:, PATCH:].astype(jnp.float32), (0, 1))]
  transfers between devices with their start and end apart: 4 -> 4, of which waited for: 4 -> 2; matrix products, arithmetic and copies ran while one was open for 0% -> 7% of each run, Pallas kernels for 0% -> 28%
where the time goes in v2:
time: 177 us
  Pallas kernels  80.4 us (45%)
  starting transfers between devices  28.8 us (16%)
  blocking collectives  21.4 us (12%)
  waiting for transfers between devices  17.6 us (10%)
  local copies, waits for them, and re-layouts  13.9 us (8%)
  matrix products  8.1 us (5%)
  other arithmetic  4.71 us (3%)
    all_to_all x4, starting transfers between devices, exchange(): return lax.all_to_all(values, AXES, split_axis=0, concat_axis=0, tiled=True)  28.8 us
    pallas_call x1, Pallas kernels, solve_users(): pl.pallas_call(functools.partial(solve_users_kernel, gram_scale), in_spec...  25.7 us
    all_to_all x1, blocking collectives, exchange(): return lax.all_to_all(values, AXES, split_axis=0, concat_axis=0, tiled=True)  21.4 us
    pallas_call x2, Pallas kernels, gather(): pl.pallas_call(functools.partial(gather_kernel, first, count, per_step),...  19.3 us
    all_to_all x4, waiting for transfers between devices, exchange(): return lax.all_to_all(values, AXES, split_axis=0, concat_axis=0, tiled=True)  17.6 us
    pallas_call x1, Pallas kernels, solve_items(): pl.pallas_call(functools.partial(solve_items_kernel, gram_scale), in_spec...  11 us
    unnamed x39, local copies, waits for them, and re-layouts  10.2 us
    pallas_call x1, Pallas kernels, bucket(): pl.pallas_call(functools.partial(bucket_kernel, batch), out_shape=(jax.Sh...  9.6 us
  transfers between devices with their start and end apart: 4, of which 2 were waited for; matrix products, arithmetic and copies ran while one was open for 7% of the time, Pallas kernels for 28%

profile of v2, /device:TPU:1, one launch (start us, length us, event | category | flops | bytes accessed | tf_op | source)
XLA Modules:
  0.0 176.6 jit_solution(14038739644521692234)
XLA Ops:
  0.6 0.0 copy-start
  0.6 0.0 copy-start.12
  0.7 4.2 %fusion.2.gram_ref = f32[128,128]{1,0:T(8,128)S(1)} fusion(f32[4096,128]{1,0:T(8,128)} %table_ref.7), kind=kOutput, calls=%fused_computation.13 | convolution fusion | flops 402653184 | bytes 2162688 | tf_op jit(solution)/shard_map/dot_general | solution.py:596
  4.9 0.0 copy-done.12
  4.9 0.0 copy-done.13
  4.9 0.0 copy-done.14
  4.9 0.0 copy-done.15
  4.9 9.6 %bucket.1 = (f32[128,256]{1,0:T(8,128)S(1)}, s32[48,128]{1,0:T(8,128)S(1)}, s32[48,128]{1,0:T(8,128)S(1)}, s32[128,128]{1,0:T(8,128)S(1)}) custom-call(s32[48,128]{1,0:T(8,128)S(1)} %bitcast.29, s32[48,128]{1,0:T(8,128)S(1)} %bitcast.30, s32[48,128]{1,0:T(8,128)S(1)} %bitcast.31, s32[48,128]{1,0:T(8,128)S(1)} %bitcast.32, f32[128,128]{1,0:T(8,128)S(1)} %fusion.2.gram_ref), custom_call_target="tpu_custom_call" | custom-call | tf_op jit(solution)/shard_map/bucket/pallas_call | solution.py:117
  14.5 0.1 copy.18
  14.6 21.4 %all_to_all.37 = f32[128,1,256]{2,1,0:T(1,128)S(1)} all-to-all(f32[128,1,256]{2,1,0:T(1,128)S(1)} %copy.18), channel_id=1, replica_groups=mesh['gx'=16,'gy'=8] {'gx','gy'}, dimensions={0} | all-to-all | bytes 262144 | tf_op jit(solution)/shard_map/all_to_all | solution.py:592
  36.1 0.0 copy-done
  36.1 10.7 %gather_rows.3 = bf16[128,64,128]{2,1,0:T(8,128)(2,1)} custom-call(s32[128,128]{1,0:T(8,128)S(1)} %get-tuple-element.156.request_ref.wanted_ref, f32[4096,128]{1,0:T(8,128)S(1)} %copy-done, f32[1,128]{1,0:T(1,128)S(1)} %bitcast.33), custom_call_target="tpu_custom_call" | custom-call | tf_op jit(solution)/shard_map/gather_rows/pallas_call | solution.py:158
  46.9 5.1 %all-to-all-start.2 = ((bf16[128,64,128]{2,1,0:T(8,128)(2,1)}), bf16[128,64,128]{2,1,0:T(8,128)(2,1)}, u32[]{:S(2)}, u32[]{:S(2)}) async-start(bf16[128,64,128]{2,1,0:T(8,128)(2,1)} %gather_rows.3), calls=%async_computation.2 | async-start | bytes 4194304 | tf_op jit(solution)/shard_map/all_to_all | solution.py:592
  51.9 3.9 %fusion.still_ref = f32[128,128]{1,0:T(8,128)S(1)} fusion(f32[4096,128]{1,0:T(8,128)} %table_ref.6), kind=kOutput, calls=%fused_computation.11 | convolution fusion | flops 383778816 | bytes 2064384 | tf_op jit(solution)/shard_map/dot_general | solution.py:596
  55.9 0.0 copy-start.1
  55.9 1.6 copy-done.1
  57.5 8.5 %gather_rows.2 = bf16[128,48,128]{2,1,0:T(8,128)(2,1)} custom-call(s32[128,128]{1,0:T(8,128)S(1)} %get-tuple-element.156.request_ref.wanted_ref, f32[4096,128]{1,0:T(8,128)S(1)} %copy-done.1), custom_call_target="tpu_custom_call" | custom-call | tf_op jit(solution)/shard_map/gather_rows/pallas_call | solution.py:158
  66.0 16.2 %all-to-all-done.2 = bf16[128,64,128]{2,1,0:T(8,128)(2,1)} async-done(((bf16[128,64,128]{2,1,0:T(8,128)(2,1)}), bf16[128,64,128]{2,1,0:T(8,128)(2,1)}, u32[]{:S(2)}, u32[]{:S(2)}) %all-to-all-start.2) | async-done | bytes 2097184 | tf_op jit(solution)/shard_map/all_to_all | solution.py:592
  82.3 5.4 %all-to-all-start.3 = ((bf16[128,48,128]{2,1,0:T(8,128)(2,1)}), bf16[128,48,128]{2,1,0:T(8,128)(2,1)}, u32[]{:S(2)}, u32[]{:S(2)}) async-start(bf16[128,48,128]{2,1,0:T(8,128)(2,1)} %gather_rows.2), calls=%async_computation.3 | async-start | bytes 3145728 | tf_op jit(solution)/shard_map/all_to_all | solution.py:592
  87.6 0.1 copy.19.count_ref
  87.7 0.0 copy-done.8
  87.7 0.0 copy-start.2
  87.7 1.6 copy-done.2
  89.3 25.7 %solve_users.1 = (f32[192,128]{1,0:T(8,128)S(1)}, bf16[128,16,128]{2,1,0:T(8,128)(2,1)}) custom-call(s32[48,128]{1,0:T(8,128)S(1)} %get-tuple-element.127.slot_ref, s32[128,128]{1,0:T(8,128)S(1)} %get-tuple-element.156.request_ref.wanted_ref, s32[48,4]{1,0:T(8,128)S(1)} %copy.19.count_ref, bf16[8192,128]{1,0:T(8,128)(2,1)} %bitcast.7.reply_ref, ...), custom_call_target="tpu_custom_call" | custom-call | tf_op jit(solution)/shard_map/solve_users/pallas_call | solution.py:423
  115.1 0.0 all-to-all-done.3
  115.1 9.9 %all-to-all-start.4 = ((bf16[128,16,128]{2,1,0:T(8,128)(2,1)}), bf16[128,16,128]{2,1,0:T(8,128)(2,1)S(1)}, u32[]{:S(2)}, u32[]{:S(2)}) async-start(bf16[128,16,128]{2,1,0:T(8,128)(2,1)} %get-tuple-element.135), calls=%async_computation.4 | async-start | bytes 1048576 | tf_op jit(solution)/shard_map/all_to_all | solution.py:592
  125.0 0.0 copy-start.17
  125.0 3.0 %slice.23 = f32[3904,128]{1,0:T(8,128)} slice(f32[4096,128]{1,0:T(8,128)} %table_ref.6), slice={[192:4096], [0:128]} | slice | bytes 3997696 | tf_op jit(solution)/shard_map/slice | solution.py:640
  128.0 0.1 copy.20.count_ref
  128.1 0.8 slice_reduce_fusion
  128.8 0.7 slice_minimum_fusion
  129.6 6.1 %unsort_rows.1.rows_ref = f32[48,128,128]{2,1,0:T(8,128)S(1)} custom-call(s32[48,128]{1,0:T(8,128)S(1)} %get-tuple-element.136.slot_ref, bf16[6144,128]{1,0:T(8,128)(2,1)} %bitcast.10.reply_ref), custom_call_target="tpu_custom_call" | custom-call | tf_op jit(solution)/shard_map/unsort_rows/pallas_call | solution.py:188
  135.7 1.6 copy-done.3
  137.3 1.4 all-to-all-done.4
  138.7 0.2 convert_reduce_fusion
  138.8 0.6 while.14
  139.5 0.7 broadcast_in_dim.23
  140.2 8.4 %all-to-all-start.5 = ((f32[128,1,128]{2,1,0:T(1,128)}), f32[128,1,128]{2,1,0:T(1,128)S(1)}, u32[]{:S(2)}, u32[]{:S(2)}) async-start(f32[128,1,128]{2,1,0:T(1,128)} %broadcast_in_dim.23), calls=%async_computation.5 | async-start | bytes 131072 | tf_op jit(solution)/shard_map/all_to_all | solution.py:592
  148.6 0.0 copy-start.10
  148.6 0.0 copy-start.11
  148.6 3.0 %pad_maximum_fusion = f32[4096,128]{1,0:T(8,128)} fusion(f32[3904,128]{1,0:T(8,128)} %slice.23, f32[192,128]{1,0:T(8,128)S(1)} %get-tuple-element.131), kind=kLoop, calls=%fused_computation.4 | loop fusion | flops 524288 | bytes 4194304 | tf_op jit(solution)/shard_map/concatenate | solution.py:654
  151.6 8.6 %build_items.1 = (bf16[48,128,128]{2,1,0:T(8,128)(2,1)S(1)}, bf16[48,128,128]{2,1,0:T(8,128)(2,1)S(1)}, f32[48,8,128]{2,1,0:T(8,128)S(1)}, f32[48,8,128]{2,1,0:T(8,128)S(1)}) custom-call(s32[128,128]{1,0:T(8,128)S(1)} %get-tuple-element.132.place_ref, s32[48,4]{1,0:T(8,128)S(1)} %copy.20.count_ref, f32[48,128,128]{2,1,0:T(8,128)} %copy-done.3, ...), custom_call_target="tpu_custom_call" | custom-call | tf_op jit(solution)/shard_map/build_items/pallas_call | solution.py:527
  160.2 1.1 copy-done.4
  161.4 1.2 copy-done.6
  162.5 0.0 all-to-all-done.5
  162.5 1.4 copy-done.5
  164.0 1.4 copy-done.7
  165.4 11.0 %solve_items.1 = f32[4096,128]{1,0:T(8,128)} custom-call(bf16[48,128,128]{2,1,0:T(8,128)(2,1)S(1)} %copy-done.5, bf16[48,128,128]{2,1,0:T(8,128)(2,1)S(1)} %copy-done.7, f32[48,8,128]{2,1,0:T(8,128)S(1)} %get-tuple-element.143.inside, f32[48,8,128]{2,1,0:T(8,128)S(1)} %get-tuple-element.144.right, f32[192,128]{1,0:T(8,128)S(1)} %slice.27.warm_ref, ...), custom_call_target="tpu_custom_call" | custom-call | tf_op jit(solution)/shard_map/solve_items/pallas_call | solution.py:579
  (20 shorter events, 0.1 us)
Async XLA Ops:
  0.6 35.5 %copy-start = (f32[4096,128]{1,0:T(8,128)S(1)}, f32[4096,128]{1,0:T(8,128)}, u32[]{:S(2)}) copy-start(f32[4096,128]{1,0:T(8,128)} %table_ref.7) | copy-start | bytes 6291460
  0.6 4.2 %copy-start.12 = (s32[6144,1]{0,1:T(1,128)S(1)}, s32[6144,1]{0,1:T(1,128)}, u32[]{:S(2)}) copy-start(s32[6144,1]{0,1:T(1,128)} %param.16) | copy-start | bytes 73732
  0.7 4.2 %copy-start.13 = (s32[6144]{0:T(1024)S(1)}, s32[6144]{0:T(1024)}, u32[]{:S(2)}) copy-start(s32[6144]{0:T(1024)} %param.17) | copy-start | bytes 73732
  0.7 4.2 %copy-start.14 = (s32[6144,1]{0,1:T(1,128)S(1)}, s32[6144,1]{0,1:T(1,128)}, u32[]{:S(2)}) copy-start(s32[6144,1]{0,1:T(1,128)} %param.21) | copy-start | bytes 73732
  0.7 4.2 %copy-start.15 = (s32[6144]{0:T(1024)S(1)}, s32[6144]{0:T(1024)}, u32[]{:S(2)}) copy-start(s32[6144]{0:T(1024)} %param.22) | copy-start | bytes 73732
  46.9 35.4 %all-to-all-start.2 = ((bf16[128,64,128]{2,1,0:T(8,128)(2,1)}), bf16[128,64,128]{2,1,0:T(8,128)(2,1)}, u32[]{:S(2)}, u32[]{:S(2)}) async-start(bf16[128,64,128]{2,1,0:T(8,128)(2,1)} %gather_rows.3), calls=%async_computation.2 | async-start | bytes 4194304 | tf_op jit(solution)/shard_map/all_to_all | solution.py:592
  55.9 1.6 copy-start.1
  66.0 21.6 %copy-start.16 = (s32[48,4]{0,1:T(4,128)S(1)}, s32[48,4]{0,1:T(4,128)}, u32[]{:S(2)}) copy-start(s32[48,4]{0,1:T(4,128)} %param.20) | copy-start | bytes 2308
  66.0 21.7 %copy-start.8 = (f32[6144]{0:T(1024)S(1)}, f32[6144]{0:T(1024)}, u32[]{:S(2)}) copy-start(f32[6144]{0:T(1024)} %param.18) | copy-start | bytes 73732
  66.0 21.7 %copy-start.9 = (f32[6144]{0:T(1024)S(1)}, f32[6144]{0:T(1024)}, u32[]{:S(2)}) copy-start(f32[6144]{0:T(1024)} %param.19) | copy-start | bytes 73732
  82.3 32.8 %all-to-all-start.3 = ((bf16[128,48,128]{2,1,0:T(8,128)(2,1)}), bf16[128,48,128]{2,1,0:T(8,128)(2,1)}, u32[]{:S(2)}, u32[]{:S(2)}) async-start(bf16[128,48,128]{2,1,0:T(8,128)(2,1)} %gather_rows.2), calls=%async_computation.3 | async-start | bytes 3145728 | tf_op jit(solution)/shard_map/all_to_all | solution.py:592
  87.7 1.6 copy-start.2
  115.1 23.6 %all-to-all-start.4 = ((bf16[128,16,128]{2,1,0:T(8,128)(2,1)}), bf16[128,16,128]{2,1,0:T(8,128)(2,1)S(1)}, u32[]{:S(2)}, u32[]{:S(2)}) async-start(bf16[128,16,128]{2,1,0:T(8,128)(2,1)} %get-tuple-element.135), calls=%async_computation.4 | async-start | bytes 1048576 | tf_op jit(solution)/shard_map/all_to_all | solution.py:592
  125.0 3.0 %copy-start.17 = (s32[48,4]{0,1:T(4,128)S(1)}, s32[48,4]{0,1:T(4,128)}, u32[]{:S(2)}) copy-start(s32[48,4]{0,1:T(4,128)} %param.25) | copy-start | bytes 2308
  135.7 1.6 copy-start.3
  140.2 22.4 %all-to-all-start.5 = ((f32[128,1,128]{2,1,0:T(1,128)}), f32[128,1,128]{2,1,0:T(1,128)S(1)}, u32[]{:S(2)}, u32[]{:S(2)}) async-start(f32[128,1,128]{2,1,0:T(1,128)} %broadcast_in_dim.23), calls=%async_computation.5 | async-start | bytes 131072 | tf_op jit(solution)/shard_map/all_to_all | solution.py:592
  148.6 3.0 %copy-start.10 = (f32[6144]{0:T(1024)S(1)}, f32[6144]{0:T(1024)}, u32[]{:S(2)}) copy-start(f32[6144]{0:T(1024)} %param.23) | copy-start | bytes 73732
  148.6 3.0 %copy-start.11 = (f32[6144]{0:T(1024)S(1)}, f32[6144]{0:T(1024)}, u32[]{:S(2)}) copy-start(f32[6144]{0:T(1024)} %param.24) | copy-start | bytes 73732
  160.2 1.1 copy-start.4
  161.4 1.2 copy-start.6
  162.5 1.4 copy-start.5
  164.0 1.4 copy-start.7

commit v3 on v2

--- a/solution.py
+++ b/solution.py
@@ -24,7 +24,18 @@
 guard_eps = 1e-06
 
 
-def bucket_kernel(batch, owner0, row0, owner1, row1, gram_ref, request_ref, slot0, slot1, place_ref):
+def bucket_kernel(batch, *refs):
+    inputs, (request_ref, slot0, slot1, place_ref) = refs[:5], refs[5:9]
+    copies = [
+        pltpu.make_async_copy(source, target, refs[14].at[k])
+        for k, (source, target) in enumerate(zip(inputs, refs[9:14]))
+    ]
+    owner0, row0, owner1, row1, table_ref = refs[9:14]
+    for copy in copies:
+        copy.start()
+    for copy in copies:
+        copy.wait()
+
     chunks = owner0.shape[0]
     sub = lax.broadcasted_iota(jnp.int32, (LANES, LANES), 0)
     lane = lax.broadcasted_iota(jnp.int32, (LANES, LANES), 1)
@@ -32,11 +43,25 @@
     prefix = jnp.concatenate([below, jnp.ones_like(below)], 1).astype(jnp.bfloat16)
     place = sub % PAD
     first_half = sub < PAD
-    group = 8
+    group = 16
     zero = jnp.zeros((LANES, LANES), jnp.float32)
+    wide = jnp.concatenate([zero, zero], 1)
+    steps = chunks // group
+    shares = [table_ref.shape[0] * part // (16 * steps) for part in (9, 6)]
+
+    def add_gram(total, start, count):
+        rows = table_ref[pl.ds(pl.multiple_of(start, LANES), count), :]
+        head = rows.astype(jnp.bfloat16)
+        rest = (rows - head.astype(jnp.float32)).astype(jnp.bfloat16)
+        return total + jnp.dot(
+            rows.T.astype(jnp.bfloat16),
+            jnp.concatenate([head, rest], 1),
+            preferred_element_type=jnp.float32,
+        )
 
     def step(half, g, state):
-        carry, wanted = state
+        carry, wanted, gram = state
+        gram = add_gram(gram, half * steps * shares[0] + g * shares[half], shares[half])
         start = pl.multiple_of(g * group, group)
         owners = (owner0, owner1)[half][pl.ds(start, group), :]
         rows = (row0, row1)[half][pl.ds(start, group), :]
@@ -65,6 +90,7 @@
         if half == 1:
             high, low = low, high
         lane_row = position.astype(jnp.float32)
+        puts = []
         for c in range(group):
             chosen = place == ranks[c : c + 1, :]
             value = jnp.where(first_half, high[c : c + 1, :], low[c : c + 1, :])
@@ -76,24 +102,26 @@
                 put = jnp.concatenate(
                     [put, jnp.where(chosen, spot, 0.0).astype(jnp.bfloat16)], 0
                 )
-            wanted = wanted + lax.dot_general(
-                hot[c].astype(jnp.bfloat16),
-                put,
-                (((1,), (1,)), ((), ())),
-                preferred_element_type=jnp.float32,
-            )
+            puts.append(put)
+        wanted = wanted + lax.dot_general(
+            jnp.concatenate(hot, 1).astype(jnp.bfloat16),
+            jnp.concatenate(puts, 1),
+            (((1,), (1,)), ((), ())),
+            preferred_element_type=jnp.float32,
+        )
         if half == 0:
             slot0[pl.ds(start, group), :] = owners * PAD + ranks
         else:
             slot1[pl.ds(start, group), :] = owners * EARLY + jnp.where(
                 ranks < PATCH, EARLY - 1, ranks - PATCH
             )
-        return carry, wanted
-
-    steps = chunks // group
-    _, first = lax.fori_loop(0, steps, functools.partial(step, 0), (zero, zero))
-    wide = jnp.concatenate([zero, zero], 1)
-    tally, second = lax.fori_loop(0, steps, functools.partial(step, 1), (zero, wide))
+        return carry, wanted, gram
+
+    _, first, gram = lax.fori_loop(0, steps, functools.partial(step, 0), (zero, zero, wide))
+    tally, second, gram = lax.fori_loop(0, steps, functools.partial(step, 1), (zero, wide, gram))
+    done = steps * sum(shares)
+    gram = add_gram(gram, done, table_ref.shape[0] - done)
+    cross = gram[:, LANES:]
     spots = second[:, LANES:]
     second = second[:, :LANES]
     first = first * PAD + pltpu.roll(first, PAD, 1)
@@ -103,7 +131,7 @@
     most = jnp.max(renewed).astype(jnp.float32)
     request = jnp.where(lane < PAD, first, second)
     request_ref[:, :LANES] = jnp.where(lane == LANES - 1, most, request)
-    request_ref[:, LANES:] = gram_ref[...]
+    request_ref[:, LANES:] = gram[:, :LANES] + cross + cross.T
     others = tally.astype(jnp.int32) // PAD
     used = (lane < renewed) | (lane >= CAP - others)
     places = jnp.where(used, spots.astype(jnp.int32), chunks * LANES)
@@ -112,19 +140,23 @@
     place_ref[...] = jnp.where(lane == PAD - 1, renewed, places)
 
 
-def bucket(owner0, row0, owner1, row1, gram, batch):
+def bucket(owner0, row0, owner1, row1, table, batch):
     slots = jax.ShapeDtypeStruct(owner0.shape, jnp.int32)
+    inputs = (owner0, row0, owner1, row1, table)
     return pl.pallas_call(
         functools.partial(bucket_kernel, batch),
+        in_specs=[pl.BlockSpec(memory_space=pltpu.HBM)] * 5,
         out_shape=(
             jax.ShapeDtypeStruct((LANES, 2 * LANES), jnp.float32),
             slots,
             slots,
             jax.ShapeDtypeStruct((LANES, LANES), jnp.int32),
         ),
+        scratch_shapes=[pltpu.VMEM(x.shape, x.dtype) for x in inputs]
+        + [pltpu.SemaphoreType.DMA((5,))],
         compiler_params=pltpu.CompilerParams(vmem_limit_bytes=32 << 20),
         name="bucket",
-    )(owner0, row0, owner1, row1, gram)
+    )(*[hold(x) for x in inputs])
 
 
 def gather_kernel(first, count, per_step, request_ref, table_ref, *refs):
@@ -189,7 +221,7 @@
         unsort_kernel,
         in_specs=[pl.BlockSpec(memory_space=pltpu.SMEM), pl.BlockSpec(memory_space=pltpu.VMEM)],
         out_specs=pl.BlockSpec(memory_space=pltpu.VMEM),
-        out_shape=pltpu.VMEM((blocks, LANES, LANES), jnp.float32),
+        out_shape=pltpu.HBM((blocks, LANES, LANES), jnp.float32),
         scratch_shapes=[pltpu.VMEM(replies.shape, jnp.float32)],
         compiler_params=pltpu.CompilerParams(vmem_limit_bytes=32 << 20),
         name="unsort_rows",
@@ -227,16 +259,18 @@
 
 
 def build_blocks(
-    first, rows, count_ref, conf_ref, rating_ref, weight_wide, turned, weighted, inside, right
+    first, rows, count_ref, conf_ref, rating_ref, weight_wide, turned, weighted, inside, right, base=None
 ):
+    base = first if base is None else base
     sub = lax.broadcasted_iota(jnp.int32, (8, LANES), 0)
     lane = lax.broadcasted_iota(jnp.int32, (8, LANES), 1)
     which = sub % 4
     sums = []
     for c, fetched in enumerate(rows):
         b = first + c
-        turned[b] = fetched.T.astype(jnp.bfloat16)
-        weighted[b] = (weight_wide[b] * fetched).astype(jnp.bfloat16)
+        pair, side = base // 2 + c // 2, pl.ds(c % 2 * LANES, LANES)
+        turned[pair, :, side] = fetched.T.astype(jnp.bfloat16)
+        weighted[pair, side, :] = (weight_wide[b] * fetched).astype(jnp.bfloat16)
         end0 = count_ref[b, 0]
         end1 = end0 + count_ref[b, 1]
         end2 = end1 + count_ref[b, 2]
@@ -244,13 +278,13 @@
         begin = jnp.where(which < 2, jnp.where(which == 0, 0, end0), jnp.where(which == 2, end1, end2))
         end = jnp.where(which < 2, jnp.where(which == 0, end0, end1), jnp.where(which == 2, end2, end3))
         mask = jnp.where((lane >= begin) & (lane < end), 1.0, 0.0)
-        inside[b] = mask
+        inside[base + c] = mask
         target = conf_ref[pl.ds(b, 1), :] * rating_ref[pl.ds(b, 1), :] * mask
         sums.append(
             jnp.dot(split(target), fetched.astype(jnp.bfloat16), preferred_element_type=jnp.float32)
         )
     for c, part in enumerate(sums):
-        right[first + c] = fold(part)
+        right[base + c] = fold(part)
 
 
 def start_from(warm_ref, x_ref, p_ref):
@@ -271,25 +305,30 @@
     gram_head = gram.astype(jnp.bfloat16)
     gram_tail = (gram - gram_head.astype(jnp.float32)).astype(jnp.bfloat16)
     gram_both = jnp.concatenate([gram_head, gram_tail], 1)
-    group = 16
+    group = 24
+    nought = jnp.zeros((8, LANES), jnp.bfloat16)
 
     def apply_system(g):
         ids = [g * group + c for c in range(group)]
         dirs = [p_ref[b] for b in ids]
         cut = [split(d) for d in dirs]
         shared = jnp.dot(jnp.concatenate(cut, 0), gram_both, preferred_element_type=jnp.float32)
-        along = [
-            fold(jnp.dot(cut[c], turned[ids[c]], preferred_element_type=jnp.float32))
-            for c in range(group)
-        ]
-        back = [
-            jnp.dot(
-                split(along[c] * inside[ids[c]]),
-                weighted[ids[c]],
+        along = []
+        for c in range(0, group, 2):
+            out = jnp.dot(
+                jnp.concatenate(cut[c : c + 2], 0),
+                turned[ids[c] // 2],
                 preferred_element_type=jnp.float32,
             )
-            for c in range(group)
-        ]
+            along += [fold(out[:8, :LANES]), fold(out[8:, LANES:])]
+        back = []
+        for c in range(0, group, 2):
+            one, two = [split(along[k] * inside[ids[k]]) for k in (c, c + 1)]
+            both = jnp.concatenate(
+                [jnp.concatenate([one, nought], 1), jnp.concatenate([nought, two], 1)], 0
+            )
+            out = jnp.dot(both, weighted[ids[c] // 2], preferred_element_type=jnp.float32)
+            back += [out[:8], out[8:]]
         images = []
         for c in range(group):
             part = shared[8 * c : 8 * c + 8]
@@ -340,7 +379,9 @@
     still_ref,
     out_ref,
     patch_ref,
+    narrow,
     wide,
+    table,
     weight_wide,
     rows,
     turned,
@@ -350,12 +391,27 @@
     r_ref,
     p_ref,
     g_ref,
+    sems,
 ):
     blocks = conf_ref.shape[0]
     batch = 4 * blocks
-    widen(reply_ref, wide)
+    parts = 4
+    depth = reply_ref.shape[0] // parts
+    fetches = []
+    for k in range(parts):
+        part = pl.ds(k * depth, depth)
+        fetches.append(pltpu.make_async_copy(reply_ref.at[part], narrow.at[part], sems.at[k]))
+        fetches[k].start()
+    load = pltpu.make_async_copy(table_ref, table, sems.at[parts])
+    load.start()
+    rest = pl.ds(batch, table_ref.shape[0] - batch)
+    keep = pltpu.make_async_copy(table.at[rest], out_ref.at[rest], sems.at[parts + 1])
     spread_weights(conf_ref, weight_wide)
     rows[...] = jnp.zeros_like(rows)
+    for k in range(parts):
+        part = pl.ds(k * depth, depth)
+        fetches[k].wait()
+        widen(narrow.at[part], wide.at[part])
 
     def build(g, state):
         first = g * TOGETHER
@@ -377,22 +433,18 @@
         return state
 
     lax.fori_loop(0, blocks // TOGETHER, build, 0)
-    start_from(table_ref, x_ref, p_ref)
+    load.wait()
+    keep.start()
+    start_from(table, x_ref, p_ref)
     gram = wide[pl.ds(CAP, LANES, stride=PAD), :] + wide[pl.ds(CAP + 1, LANES, stride=PAD), :]
     conjugate(gram * gram_scale, turned, weighted, inside, x_ref, r_ref, p_ref, g_ref)
-    give(x_ref, out_ref)
-
-    table = wide.at[pl.ds(0, table_ref.shape[0])]
-    solved = out_ref[...]
-    table[pl.ds(0, batch), :] = solved
-    step = 64
-
-    def copy(i, state):
-        start = pl.multiple_of(batch + i * step, step)
-        table[pl.ds(start, step), :] = table_ref[pl.ds(start, step), :]
-        return state
-
-    lax.fori_loop(0, (table_ref.shape[0] - batch) // step, copy, 0)
+    give(x_ref, table)
+    put = pltpu.make_async_copy(
+        table.at[pl.ds(0, batch)], out_ref.at[pl.ds(0, batch)], sems.at[parts + 2]
+    )
+    put.start()
+
+    solved = table[pl.ds(0, batch), :]
     head = solved.astype(jnp.bfloat16)
     rest = (solved - head.astype(jnp.float32)).astype(jnp.bfloat16)
     head_turned = head.astype(jnp.float32).T.astype(jnp.bfloat16)
@@ -412,33 +464,42 @@
         return state
 
     lax.fori_loop(0, wanted_ref.shape[0], one, 0)
+    put.wait()
+    keep.wait()
 
 
 def solve_users(slots, wanted, counts, replies, confidence, rating, table, still, gram_scale):
     blocks = confidence.shape[0]
     vmem = pl.BlockSpec(memory_space=pltpu.VMEM)
     smem = pl.BlockSpec(memory_space=pltpu.SMEM)
-    state = pltpu.VMEM((blocks, 8, LANES), jnp.float32)
-    matrices = pltpu.VMEM((blocks, LANES, LANES), jnp.bfloat16)
+    hbm = pl.BlockSpec(memory_space=pltpu.HBM)
     return pl.pallas_call(
         functools.partial(solve_users_kernel, gram_scale),
-        in_specs=[smem] * 3 + [vmem] * 5,
-        out_specs=[vmem, vmem],
+        in_specs=[smem, smem, smem, hbm, vmem, vmem, hbm, vmem],
+        out_specs=[hbm, vmem],
         out_shape=[
-            jax.ShapeDtypeStruct((4 * blocks, LANES), jnp.float32),
+            jax.ShapeDtypeStruct(table.shape, jnp.float32),
             pltpu.HBM((wanted.shape[0], SLOT, LANES), jnp.bfloat16),
         ],
         scratch_shapes=[
+            pltpu.VMEM(replies.shape, jnp.bfloat16),
             pltpu.VMEM(replies.shape, jnp.float32),
+            pltpu.VMEM(table.shape, jnp.float32),
             pltpu.VMEM((blocks, LANES, LANES), jnp.float32),
             pltpu.VMEM((TOGETHER, LANES, LANES), jnp.float32),
-            matrices,
-            matrices,
         ]
-        + [state] * 5,
+        + matrices(blocks)
+        + [pltpu.SemaphoreType.DMA((7,))],
         compiler_params=pltpu.CompilerParams(vmem_limit_bytes=48 << 20),
         name="solve_users",
-    )(slots, wanted, counts, replies, confidence, rating, table, still)
+    )(slots, wanted, counts, hold(replies), confidence, rating, hold(table), still)
+
+
+def matrices(blocks):
+    return [
+        pltpu.VMEM((blocks // 2, LANES, 2 * LANES), jnp.bfloat16),
+        pltpu.VMEM((blocks // 2, 2 * LANES, LANES), jnp.bfloat16),
+    ] + [pltpu.VMEM((blocks, 8, LANES), jnp.float32)] * 5
 
 
 def build_items_kernel(
@@ -458,17 +519,8 @@
     more_wide,
     weight_wide,
     rows,
+    sem,
 ):
-    blocks = conf_ref.shape[0]
-    widen(patch_ref, wide)
-    spread_weights(conf_ref, weight_wide)
-
-    def copy(b, state):
-        rows[pl.ds(pl.multiple_of(b * LANES, LANES), LANES), :] = rows_ref[b]
-        return state
-
-    lax.fori_loop(0, blocks, copy, 0)
-
     def renew(o, state):
         def put(k):
             rows[pl.ds(place_ref[o, k], 1), :] = wide[pl.ds(o * SLOT + k, 1), :]
@@ -496,96 +548,111 @@
 
         return state
 
-    lax.fori_loop(0, place_ref.shape[0], renew, 0)
-
-    def build(g, state):
-        first = g * TOGETHER
-        start = pl.multiple_of(first * LANES, LANES)
-        build_blocks(
-            first,
-            [rows[pl.ds(start + c * LANES, LANES), :] for c in range(TOGETHER)],
-            count_ref,
-            conf_ref,
-            rating_ref,
-            weight_wide,
-            turned,
-            weighted,
-            inside,
-            right,
-        )
-        return state
-
-    lax.fori_loop(0, blocks // TOGETHER, build, 0)
+    @pl.when(pl.program_id(0) == 0)
+    def _():
+        load = pltpu.make_async_copy(rows_ref, rows.at[pl.ds(0, rows_ref.shape[0])], sem)
+        load.start()
+        widen(patch_ref, wide)
+        spread_weights(conf_ref, weight_wide)
+        load.wait()
+        lax.fori_loop(0, place_ref.shape[0], renew, 0)
+
+    first = pl.program_id(0) * TOGETHER
+    start = pl.multiple_of(first * LANES, LANES)
+    build_blocks(
+        first,
+        [rows[pl.ds(start + c * LANES, LANES), :] for c in range(TOGETHER)],
+        count_ref,
+        conf_ref,
+        rating_ref,
+        weight_wide,
+        turned,
+        weighted,
+        inside,
+        right,
+        0,
+    )
 
 
 def build_items(places, counts, rows, patch, more, confidence, rating):
     blocks = confidence.shape[0]
     vmem = pl.BlockSpec(memory_space=pltpu.VMEM)
     smem = pl.BlockSpec(memory_space=pltpu.SMEM)
-    matrices = pltpu.VMEM((blocks, LANES, LANES), jnp.bfloat16)
-    vectors = pltpu.VMEM((blocks, 8, LANES), jnp.float32)
+    hbm = pl.BlockSpec(memory_space=pltpu.HBM)
+    pairs = TOGETHER // 2
+    shapes = [
+        ((blocks // 2, LANES, 2 * LANES), jnp.bfloat16, pairs),
+        ((blocks // 2, 2 * LANES, LANES), jnp.bfloat16, pairs),
+        ((blocks, 8, LANES), jnp.float32, TOGETHER),
+        ((blocks, 8, LANES), jnp.float32, TOGETHER),
+    ]
     return pl.pallas_call(
         build_items_kernel,
-        in_specs=[smem] * 2 + [vmem] * 2 + [pl.BlockSpec(memory_space=pl.ANY)] + [vmem] * 2,
-        out_specs=[vmem] * 4,
-        out_shape=[matrices, matrices, vectors, vectors],
+        grid=(blocks // TOGETHER,),
+        in_specs=[smem, smem, hbm, vmem, hbm, vmem, vmem],
+        out_specs=[
+            pl.BlockSpec((step,) + shape[1:], lambda i: (i, 0, 0)) for shape, _, step in shapes
+        ],
+        out_shape=[pltpu.HBM(shape, kind) for shape, kind, _ in shapes],
         scratch_shapes=[
             pltpu.VMEM(patch.shape, jnp.float32),
             pltpu.VMEM(more.shape[1:], jnp.bfloat16),
             pltpu.VMEM(more.shape[1:], jnp.float32),
             pltpu.VMEM((blocks, LANES, LANES), jnp.float32),
             pltpu.VMEM((blocks * LANES + 8, LANES), jnp.float32),
+            pltpu.SemaphoreType.DMA,
         ],
         compiler_params=pltpu.CompilerParams(vmem_limit_bytes=48 << 20),
         name="build_items",
-    )(places, counts, rows, patch, more, confidence, rating)
-
-
-def solve_items_kernel(
-    gram_scale,
-    turned,
-    weighted,
-    inside,
-    right,
-    warm_ref,
-    gram_ref,
-    table_ref,
-    out_ref,
-    x_ref,
-    r_ref,
-    p_ref,
-    g_ref,
-    solved,
-    sems,
-):
-    batch = solved.shape[0]
-    rest = pl.ds(batch, table_ref.shape[0] - batch)
-    keep = pltpu.make_async_copy(table_ref.at[rest], out_ref.at[rest], sems.at[0])
+    )(places, counts, hold(rows), patch, hold(more), confidence, rating)
+
+
+def solve_items_kernel(gram_scale, *refs):
+    built, (gram_ref, table_ref, out_ref, table) = refs[:4], refs[4:8]
+    turned, weighted, inside, x_ref, r_ref, p_ref, g_ref, sems = refs[8:]
+    loads = [
+        pltpu.make_async_copy(source, target, sems.at[k])
+        for k, (source, target) in enumerate(zip(built, (turned, weighted, inside, r_ref)))
+    ]
+    for load in loads:
+        load.start()
+    loads.append(pltpu.make_async_copy(table_ref, table, sems.at[4]))
+    loads[4].start()
+    batch = 4 * x_ref.shape[0]
+    rest = pl.ds(batch, table.shape[0] - batch)
+    keep = pltpu.make_async_copy(table.at[rest], out_ref.at[rest], sems.at[5])
+    for load in loads:
+        load.wait()
     keep.start()
-    start_from(warm_ref, x_ref, p_ref)
-    r_ref[...] = right[...]
+    start_from(table, x_ref, p_ref)
     conjugate(gram_ref[...] * gram_scale, turned, weighted, inside, x_ref, r_ref, p_ref, g_ref)
-    give(x_ref, solved)
-    put = pltpu.make_async_copy(solved, out_ref.at[pl.ds(0, batch)], sems.at[1])
+    give(x_ref, table)
+    first = pl.ds(0, batch)
+    put = pltpu.make_async_copy(table.at[first], out_ref.at[first], sems.at[6])
     put.start()
     put.wait()
     keep.wait()
 
 
 def solve_items(built, table, gram, gram_scale):
-    blocks = built[0].shape[0]
+    blocks = built[2].shape[0]
     vmem = pl.BlockSpec(memory_space=pltpu.VMEM)
     hbm = pl.BlockSpec(memory_space=pltpu.HBM)
     return pl.pallas_call(
         functools.partial(solve_items_kernel, gram_scale),
-        in_specs=[vmem] * 6 + [hbm],
+        in_specs=[hbm] * 4 + [vmem, hbm],
         out_specs=hbm,
         out_shape=jax.ShapeDtypeStruct(table.shape, jnp.float32),
-        scratch_shapes=[pltpu.VMEM((blocks, 8, LANES), jnp.float32)] * 4
-        + [pltpu.VMEM((4 * blocks, LANES), jnp.float32), pltpu.SemaphoreType.DMA((2,))],
-        compiler_params=pltpu.CompilerParams(vmem_limit_bytes=32 << 20),
+        scratch_shapes=[pltpu.VMEM(table.shape, jnp.float32)]
+        + matrices(blocks)
+        + [pltpu.SemaphoreType.DMA((7,))],
+        compiler_params=pltpu.CompilerParams(vmem_limit_bytes=48 << 20),
         name="solve_items",
-    )(*built, table[: 4 * blocks], gram, table)
+    )(*[hold(x) for x in built], gram, hold(table))
+
+
+def hold(values):
+    return pltpu.with_memory_space_constraint(values, pltpu.HBM)
 
 
 def exchange(values):
@@ -626,7 +693,7 @@
         by_block(item_row),
         by_block(user_owner),
         by_block(user_row),
-        local_gram(item_table),
+        item_table,
         batch,
     )
     came = exchange(requests[:, None, :])[:, 0]
@@ -640,7 +707,7 @@
     still = local_gram(user_table[batch:])
     early, still, replies = lax.optimization_barrier((early, still, replies))
     early = exchange(early)
-    renewed, patch = solve_users(
+    new_users, patch = solve_users(
         item_slots,
         wanted,
         user_counts,
@@ -651,14 +718,12 @@
         still,
         gram_scale,
     )
-    new_users = jnp.concatenate([renewed, user_table[batch:]], 0)
-
     patch, early = lax.optimization_barrier((patch, early))
     patch = exchange(patch)
-    narrow = renewed.astype(jnp.bfloat16)
 
     def another(state):
         done, kept = state
+        narrow = new_users[:batch].astype(jnp.bfloat16)
         rows = narrow[lax.dynamic_slice_in_dim(fresh, done, SLOT, 1)]
         return done + SLOT, lax.dynamic_update_slice(kept, exchange(rows), (0, done - PATCH, 0))
 
@@ -670,7 +735,7 @@
     built = build_items(
         places,
         item_counts,
-        rows,
+        rows.reshape(-1, width),
         patch.reshape(-1, width),
         more,
         by_block(item_confidence),

time: 177 us -> 157 us (0.89)
  local copies, waits for them, and re-layouts: 13.9 us -> 1.93 us
  waiting for transfers between devices: 17.6 us -> 27.3 us
  starting transfers between devices: 28.8 us -> 21.9 us
  matrix products: 8.1 us -> 1.78 us
  other arithmetic: 4.71 us -> 1.01 us
    unnamed x39 -> x19, local copies, waits for them, and re-layouts: 10.2 us -> 0.23 us
    all_to_all x4, waiting for transfers between devices: 17.6 us -> 27.3 us  [exchange(): return lax.all_to_all(values, AXES, split_axis=0, concat_axis=0, tiled=True)]
    all_to_all x4, starting transfers between devices: 28.8 us -> 21.9 us  [exchange(): return lax.all_to_all(values, AXES, split_axis=0, concat_axis=0, tiled=True)]
    dot_general x2 -> x1, matrix products: 8.1 us -> 1.78 us  [local_gram(): jnp.dot(table.T, table, precision=lax.Precision.HIGH, preferred_element_t...]
    pallas_call x1, Pallas kernels: 25.7 us -> 22.3 us  [solve_users(): pl.pallas_call(functools.partial(solve_users_kernel, gram_scale), in_spec...]
    concatenate x1 -> x0, other arithmetic: 3.02 us -> none  [shards(): new_users = jnp.concatenate([renewed, user_table[batch:]], 0)]
    slice x2 -> x1, local copies, waits for them, and re-layouts: 2.98 us -> 0.9 us  [another(): narrow = new_users[:batch].astype(jnp.bfloat16)]
    pallas_call x2, Pallas kernels: 18.2 us -> 20.1 us  [the longest x1 12.2 us: build_items(): pl.pallas_call(build_items_kernel, grid=(blocks // TOGETHER,), in_specs=[...]
  transfers between devices with their start and end apart: 4 -> 4, of which waited for: 2 -> 3; matrix products, arithmetic and copies ran while one was open for 7% -> 2% of each run, Pallas kernels for 28% -> 32%
where the time goes in v3:
time: 157 us; the launch traced here: 156 us
  Pallas kernels  79.5 us (51%)
  waiting for transfers between devices  27.3 us (17%)
  starting transfers between devices  21.9 us (14%)
  blocking collectives  21.4 us (14%)
  local copies, waits for them, and re-layouts  1.93 us (1%)
  matrix products  1.78 us (1%)
    all_to_all x4, waiting for transfers between devices, exchange(): return lax.all_to_all(values, AXES, split_axis=0, concat_axis=0, tiled=True)  27.3 us
    pallas_call x1, Pallas kernels, solve_users(): pl.pallas_call(functools.partial(solve_users_kernel, gram_scale), in_spec...  22.3 us
    all_to_all x4, starting transfers between devices, exchange(): return lax.all_to_all(values, AXES, split_axis=0, concat_axis=0, tiled=True)  21.9 us
    all_to_all x1, blocking collectives, exchange(): return lax.all_to_all(values, AXES, split_axis=0, concat_axis=0, tiled=True)  21.4 us
    pallas_call x2, Pallas kernels, gather(): pl.pallas_call(functools.partial(gather_kernel, first, count, per_step),...  19.3 us
    pallas_call x1, Pallas kernels, build_items(): pl.pallas_call(build_items_kernel, grid=(blocks // TOGETHER,), in_specs=[...  12.2 us
    pallas_call x1, Pallas kernels, solve_items(): pl.pallas_call(functools.partial(solve_items_kernel, gram_scale), in_spec...  10.5 us
    pallas_call x1, Pallas kernels, bucket(): pl.pallas_call(functools.partial(bucket_kernel, batch), in_specs=[pl.Bloc...  7.82 us
  transfers between devices with their start and end apart: 4, of which 3 were waited for; matrix products, arithmetic and copies ran while one was open for 2% of the time, Pallas kernels for 32%

profile of v3, /device:TPU:1, one launch (start us, length us, event | category | flops | bytes accessed | tf_op | source)
XLA Modules:
  0.0 156.2 jit_solution(8384266685617325833)
XLA Ops:
  0.6 0.0 copy-start
  0.6 7.8 %bucket.1 = (f32[128,256]{1,0:T(8,128)S(1)}, s32[48,128]{1,0:T(8,128)S(1)}, s32[48,128]{1,0:T(8,128)S(1)}, s32[128,128]{1,0:T(8,128)S(1)}) custom-call(s32[48,128]{1,0:T(8,128)} %bitcast.32, s32[48,128]{1,0:T(8,128)} %bitcast.33, s32[48,128]{1,0:T(8,128)} %bitcast.34, s32[48,128]{1,0:T(8,128)} %bitcast.35, f32[4096,128]{1,0:T(8,128)} %refs_5_.1), custom_call_target="tpu_custom_call" | custom-call | tf_op jit(solution)/shard_map/bucket/pallas_call | solution.py:146
  8.5 0.1 copy.18
  8.6 21.4 %all_to_all.37 = f32[128,1,256]{2,1,0:T(1,128)S(1)} all-to-all(f32[128,1,256]{2,1,0:T(1,128)S(1)} %copy.18), channel_id=1, replica_groups=mesh['gx'=16,'gy'=8] {'gx','gy'}, dimensions={0} | all-to-all | bytes 262144 | tf_op jit(solution)/shard_map/all_to_all | solution.py:659
  30.1 0.0 copy-done
  30.1 10.7 %gather_rows.3 = bf16[128,64,128]{2,1,0:T(8,128)(2,1)} custom-call(s32[128,128]{1,0:T(8,128)S(1)} %get-tuple-element.158.request_ref.wanted_ref, f32[4096,128]{1,0:T(8,128)S(1)} %copy-done, f32[1,128]{1,0:T(1,128)S(1)} %bitcast.29), custom_call_target="tpu_custom_call" | custom-call | tf_op jit(solution)/shard_map/gather_rows/pallas_call | solution.py:190
  40.8 0.0 copy-start.1
  40.8 5.2 %all-to-all-start.2 = ((bf16[128,64,128]{2,1,0:T(8,128)(2,1)}), bf16[128,64,128]{2,1,0:T(8,128)(2,1)}, u32[]{:S(2)}, u32[]{:S(2)}) async-start(bf16[128,64,128]{2,1,0:T(8,128)(2,1)} %gather_rows.3), calls=%async_computation.2 | async-start | bytes 4194304 | tf_op jit(solution)/shard_map/all_to_all | solution.py:659
  46.1 0.0 copy-done.1
  46.1 1.8 %fusion.still_ref = f32[128,128]{1,0:T(8,128)S(1)} fusion(f32[4096,128]{1,0:T(8,128)S(1)} %copy-done.1), kind=kOutput, calls=%fused_computation.4 | convolution fusion | flops 383778816 | bytes 2064384 | tf_op jit(solution)/shard_map/dot_general | solution.py:663
  47.9 8.6 %gather_rows.2 = bf16[128,48,128]{2,1,0:T(8,128)(2,1)} custom-call(s32[128,128]{1,0:T(8,128)S(1)} %get-tuple-element.158.request_ref.wanted_ref, f32[4096,128]{1,0:T(8,128)S(1)} %copy-done.1), custom_call_target="tpu_custom_call" | custom-call | tf_op jit(solution)/shard_map/gather_rows/pallas_call | solution.py:190
  56.4 0.0 copy-start.6
  56.5 0.0 copy-start.2
  56.5 0.0 copy-start.3
  56.5 19.9 %all-to-all-done.2 = bf16[128,64,128]{2,1,0:T(8,128)(2,1)} async-done(((bf16[128,64,128]{2,1,0:T(8,128)(2,1)}), bf16[128,64,128]{2,1,0:T(8,128)(2,1)}, u32[]{:S(2)}, u32[]{:S(2)}) %all-to-all-start.2) | async-done | bytes 2097184 | tf_op jit(solution)/shard_map/all_to_all | solution.py:659
  76.4 4.4 %all-to-all-start.3 = ((bf16[128,48,128]{2,1,0:T(8,128)(2,1)}), bf16[128,48,128]{2,1,0:T(8,128)(2,1)S(1)}, u32[]{:S(2)}, u32[]{:S(2)}) async-start(bf16[128,48,128]{2,1,0:T(8,128)(2,1)} %gather_rows.2), calls=%async_computation.3 | async-start | bytes 3145728 | tf_op jit(solution)/shard_map/all_to_all | solution.py:659
  80.7 0.0 copy-done.6
  80.7 0.1 copy.19.count_ref
  80.8 0.0 copy-done.2
  80.8 0.0 copy-done.3
  80.8 22.3 %solve_users.1 = (f32[4096,128]{1,0:T(8,128)}, bf16[128,16,128]{2,1,0:T(8,128)(2,1)}) custom-call(s32[48,128]{1,0:T(8,128)S(1)} %get-tuple-element.129.slot_ref, s32[128,128]{1,0:T(8,128)S(1)} %get-tuple-element.158.request_ref.wanted_ref, s32[48,4]{1,0:T(8,128)S(1)} %copy.19.count_ref, bf16[8192,128]{1,0:T(8,128)(2,1)} %bitcast.7.reply_ref, ...), custom_call_target="tpu_custom_call" | custom-call | tf_op jit(solution)/shard_map/solve_users/pallas_call | solution.py:476
  103.2 2.6 %all-to-all-done.3 = bf16[128,48,128]{2,1,0:T(8,128)(2,1)S(1)} async-done(((bf16[128,48,128]{2,1,0:T(8,128)(2,1)}), bf16[128,48,128]{2,1,0:T(8,128)(2,1)S(1)}, u32[]{:S(2)}, u32[]{:S(2)}) %all-to-all-start.3) | async-done | bytes 1572896 | tf_op jit(solution)/shard_map/all_to_all | solution.py:659
  105.8 7.3 %all-to-all-start.4 = ((bf16[128,16,128]{2,1,0:T(8,128)(2,1)}), bf16[128,16,128]{2,1,0:T(8,128)(2,1)S(1)}, u32[]{:S(2)}, u32[]{:S(2)}) async-start(bf16[128,16,128]{2,1,0:T(8,128)(2,1)} %get-tuple-element.137), calls=%async_computation.4 | async-start | bytes 1048576 | tf_op jit(solution)/shard_map/all_to_all | solution.py:659
  113.1 0.7 slice_reduce_fusion
  113.8 0.1 slice_minimum_fusion
  113.9 0.9 slice.46
  114.8 7.3 %unsort_rows.1 = f32[48,128,128]{2,1,0:T(8,128)} custom-call(s32[48,128]{1,0:T(8,128)S(1)} %get-tuple-element.138.slot_ref, bf16[6144,128]{1,0:T(8,128)(2,1)S(1)} %bitcast.21), custom_call_target="tpu_custom_call" | custom-call | tf_op jit(solution)/shard_map/unsort_rows/pallas_call | solution.py:220
  122.1 4.7 %all-to-all-done.4 = bf16[128,16,128]{2,1,0:T(8,128)(2,1)S(1)} async-done(((bf16[128,16,128]{2,1,0:T(8,128)(2,1)}), bf16[128,16,128]{2,1,0:T(8,128)(2,1)S(1)}, u32[]{:S(2)}, u32[]{:S(2)}) %all-to-all-start.4) | async-done | bytes 524320 | tf_op jit(solution)/shard_map/all_to_all | solution.py:659
  126.8 0.2 convert_reduce_fusion
  126.9 0.0 copy-start.7
  126.9 0.0 copy-start.4
  127.0 0.0 copy-start.5
  127.0 0.7 while.14
  127.6 0.7 broadcast_in_dim.23
  128.3 5.1 %all-to-all-start.5 = ((f32[128,1,128]{2,1,0:T(1,128)}), f32[128,1,128]{2,1,0:T(1,128)S(1)}, u32[]{:S(2)}, u32[]{:S(2)}) async-start(f32[128,1,128]{2,1,0:T(1,128)} %broadcast_in_dim.23), calls=%async_computation.5 | async-start | bytes 131072 | tf_op jit(solution)/shard_map/all_to_all | solution.py:659
  133.4 0.0 copy-done.7
  133.4 0.1 copy.20.count_ref
  133.5 0.0 copy-done.4
  133.5 0.0 copy-done.5
  133.5 12.2 %build_items.1 = (bf16[24,128,256]{2,1,0:T(8,128)(2,1)}, bf16[24,256,128]{2,1,0:T(8,128)(2,1)}, f32[48,8,128]{2,1,0:T(8,128)}, f32[48,8,128]{2,1,0:T(8,128)}) custom-call(s32[128,128]{1,0:T(8,128)S(1)} %get-tuple-element.134.place_ref, s32[48,4]{1,0:T(8,128)S(1)} %copy.20.count_ref, f32[6144,128]{1,0:T(8,128)} %bitcast.30, bf16[2048,128]{1,0:T(8,128)(2,1)S(1)} %bitcast.22, ...), custom_call_target="tpu_custom_call" | custom-call | tf_op jit(solution)/shard_map/build_items/pallas_call | solution.py:589
  145.7 0.0 all-to-all-done.5
  145.7 10.5 %solve_items.1 = f32[4096,128]{1,0:T(8,128)} custom-call(bf16[24,128,256]{2,1,0:T(8,128)(2,1)} %get-tuple-element.143.refs_0_, bf16[24,256,128]{2,1,0:T(8,128)(2,1)} %get-tuple-element.144.refs_1_, f32[48,8,128]{2,1,0:T(8,128)} %get-tuple-element.145.refs_2_, f32[48,8,128]{2,1,0:T(8,128)} %get-tuple-element.146.refs_3_, f32[128,128]{1,0:T(8,128)S(1)} %bitcast.23, ...), custom_call_target="tpu_custom_call" | custom-call | tf_op jit(solution)/shard_map/solve_items/pallas_call | solution.py:641
  (2 shorter events, 0.0 us)
Async XLA Ops:
  0.6 29.5 %copy-start = (f32[4096,128]{1,0:T(8,128)S(1)}, f32[4096,128]{1,0:T(8,128)}, u32[]{:S(2)}) copy-start(f32[4096,128]{1,0:T(8,128)} %refs_5_.1) | copy-start | bytes 6291460
  40.8 5.3 %copy-start.1 = (f32[4096,128]{1,0:T(8,128)S(1)}, f32[4096,128]{1,0:T(8,128)}, u32[]{:S(2)}) copy-start(f32[4096,128]{1,0:T(8,128)} %table_ref.5) | copy-start | bytes 6291460
  40.8 35.6 %all-to-all-start.2 = ((bf16[128,64,128]{2,1,0:T(8,128)(2,1)}), bf16[128,64,128]{2,1,0:T(8,128)(2,1)}, u32[]{:S(2)}, u32[]{:S(2)}) async-start(bf16[128,64,128]{2,1,0:T(8,128)(2,1)} %gather_rows.3), calls=%async_computation.2 | async-start | bytes 4194304 | tf_op jit(solution)/shard_map/all_to_all | solution.py:659
  56.4 24.3 %copy-start.6 = (s32[48,4]{0,1:T(4,128)S(1)}, s32[48,4]{0,1:T(4,128)}, u32[]{:S(2)}) copy-start(s32[48,4]{0,1:T(4,128)} %param.20) | copy-start | bytes 2308
  56.5 24.4 %copy-start.2 = (f32[6144]{0:T(1024)S(1)}, f32[6144]{0:T(1024)}, u32[]{:S(2)}) copy-start(f32[6144]{0:T(1024)} %param.18) | copy-start | bytes 73732
  56.5 24.4 %copy-start.3 = (f32[6144]{0:T(1024)S(1)}, f32[6144]{0:T(1024)}, u32[]{:S(2)}) copy-start(f32[6144]{0:T(1024)} %param.19) | copy-start | bytes 73732
  76.4 29.4 %all-to-all-start.3 = ((bf16[128,48,128]{2,1,0:T(8,128)(2,1)}), bf16[128,48,128]{2,1,0:T(8,128)(2,1)S(1)}, u32[]{:S(2)}, u32[]{:S(2)}) async-start(bf16[128,48,128]{2,1,0:T(8,128)(2,1)} %gather_rows.2), calls=%async_computation.3 | async-start | bytes 3145728 | tf_op jit(solution)/shard_map/all_to_all | solution.py:659
  105.8 21.0 %all-to-all-start.4 = ((bf16[128,16,128]{2,1,0:T(8,128)(2,1)}), bf16[128,16,128]{2,1,0:T(8,128)(2,1)S(1)}, u32[]{:S(2)}, u32[]{:S(2)}) async-start(bf16[128,16,128]{2,1,0:T(8,128)(2,1)} %get-tuple-element.137), calls=%async_computation.4 | async-start | bytes 1048576 | tf_op jit(solution)/shard_map/all_to_all | solution.py:659
  126.9 6.4 %copy-start.7 = (s32[48,4]{0,1:T(4,128)S(1)}, s32[48,4]{0,1:T(4,128)}, u32[]{:S(2)}) copy-start(s32[48,4]{0,1:T(4,128)} %param.25) | copy-start | bytes 2308
  126.9 6.5 %copy-start.4 = (f32[6144]{0:T(1024)S(1)}, f32[6144]{0:T(1024)}, u32[]{:S(2)}) copy-start(f32[6144]{0:T(1024)} %param.23) | copy-start | bytes 73732
  127.0 6.5 %copy-start.5 = (f32[6144]{0:T(1024)S(1)}, f32[6144]{0:T(1024)}, u32[]{:S(2)}) copy-start(f32[6144]{0:T(1024)} %param.24) | copy-start | bytes 73732
  128.3 17.4 %all-to-all-start.5 = ((f32[128,1,128]{2,1,0:T(1,128)}), f32[128,1,128]{2,1,0:T(1,128)S(1)}, u32[]{:S(2)}, u32[]{:S(2)}) async-start(f32[128,1,128]{2,1,0:T(1,128)} %broadcast_in_dim.23), calls=%async_computation.5 | async-start | bytes 131072 | tf_op jit(solution)/shard_map/all_to_all | solution.py:659

commit v4 on v3

--- a/solution.py
+++ b/solution.py
@@ -15,8 +15,8 @@
 PATCH = 14
 SLOT = 16
 EARLY = 48
-EAGER = 6
 TOGETHER = 4
+STRIDE = 12
 LANES = 128
 
 ridge_weight = 1.0
@@ -43,7 +43,7 @@
     prefix = jnp.concatenate([below, jnp.ones_like(below)], 1).astype(jnp.bfloat16)
     place = sub % PAD
     first_half = sub < PAD
-    group = 16
+    group = 24
     zero = jnp.zeros((LANES, LANES), jnp.float32)
     wide = jnp.concatenate([zero, zero], 1)
     steps = chunks // group
@@ -135,8 +135,7 @@
     others = tally.astype(jnp.int32) // PAD
     used = (lane < renewed) | (lane >= CAP - others)
     places = jnp.where(used, spots.astype(jnp.int32), chunks * LANES)
-    looked = jnp.where(others > CAP - PATCH, PATCH, jnp.minimum(renewed, PATCH))
-    places = jnp.where(lane == PAD - 2, looked, places)
+    places = jnp.where(lane == PAD - 2, most.astype(jnp.int32), places)
     place_ref[...] = jnp.where(lane == PAD - 1, renewed, places)
 
 
@@ -171,11 +170,18 @@
     for k in range(2):
         wide[k, count:, :] = last
 
+    sub = lax.broadcasted_iota(jnp.int32, (8, LANES), 0)
+
     def one(s, state):
         buffer = wide.at[s % 2]
-        for i in range(count):
-            index = request_ref[base + s, first + i]
-            buffer[pl.ds(i, 1), :] = table_ref[pl.ds(index, 1), :]
+        for q in range(0, count, 8):
+            part = None
+            for i in range(min(8, count - q)):
+                index = request_ref[base + s, first + q + i]
+                row = jnp.broadcast_to(table_ref[pl.ds(index, 1), :], (8, LANES))
+                part = row if part is None else jnp.where(sub == i, row, part)
+            height = min(8, count - q)
+            buffer[pl.ds(q, height), :] = part[:height]
         out_ref[s] = buffer[...].astype(jnp.bfloat16)
         return state
 
@@ -269,7 +275,7 @@
     for c, fetched in enumerate(rows):
         b = first + c
         pair, side = base // 2 + c // 2, pl.ds(c % 2 * LANES, LANES)
-        turned[pair, :, side] = fetched.T.astype(jnp.bfloat16)
+        turned[pair, :, side] = fetched.astype(jnp.bfloat16).T
         weighted[pair, side, :] = (weight_wide[b] * fetched).astype(jnp.bfloat16)
         end0 = count_ref[b, 0]
         end1 = end0 + count_ref[b, 1]
@@ -300,7 +306,7 @@
         out_ref[pl.ds(4 * b, 4), :] = x_ref[b, :4, :]
 
 
-def conjugate(gram, turned, weighted, inside, x_ref, r_ref, p_ref, g_ref):
+def conjugate(gram, turned, weighted, inside, x_ref, r_ref, p_ref, g_ref, midway=None):
     blocks = x_ref.shape[0]
     gram_head = gram.astype(jnp.bfloat16)
     gram_tail = (gram - gram_head.astype(jnp.float32)).astype(jnp.bfloat16)
@@ -346,6 +352,9 @@
             g_ref[ids[c]] = jnp.broadcast_to(
                 jnp.sum(resid * resid, -1, keepdims=True), (8, LANES)
             )
+
+    if midway is not None:
+        midway()
 
     def iterate(i, state):
         for g in range(blocks // group):
@@ -522,17 +531,11 @@
     sem,
 ):
     def renew(o, state):
-        def put(k):
+        for k in range(PATCH):
             rows[pl.ds(place_ref[o, k], 1), :] = wide[pl.ds(o * SLOT + k, 1), :]
-
-        for k in range(EAGER):
-            put(k)
-
-        @pl.when(place_ref[o, PAD - 2] > EAGER)
-        def _():
-            for k in range(EAGER, PATCH):
-                put(k)
-
+        return state
+
+    def renew_more(o, state):
         count = place_ref[o, PAD - 1]
 
         @pl.when(count > PATCH)
@@ -540,11 +543,11 @@
             pltpu.sync_copy(more_ref.at[o], more_narrow)
             more_wide[...] = more_narrow[...].astype(jnp.float32)
 
-            def put_more(k, inner):
+            def put(k, inner):
                 rows[pl.ds(place_ref[o, k], 1), :] = more_wide[pl.ds(k - PATCH, 1), :]
                 return inner
 
-            lax.fori_loop(PATCH, count, put_more, 0)
+            lax.fori_loop(PATCH, count, put, 0)
 
         return state
 
@@ -555,13 +558,17 @@
         widen(patch_ref, wide)
         spread_weights(conf_ref, weight_wide)
         load.wait()
-        lax.fori_loop(0, place_ref.shape[0], renew, 0)
-
-    first = pl.program_id(0) * TOGETHER
+        lax.fori_loop(0, place_ref.shape[0], renew, 0, unroll=4)
+
+        @pl.when(place_ref[0, PAD - 2] > PATCH)
+        def _():
+            lax.fori_loop(0, place_ref.shape[0], renew_more, 0)
+
+    first = pl.program_id(0) * STRIDE
     start = pl.multiple_of(first * LANES, LANES)
     build_blocks(
         first,
-        [rows[pl.ds(start + c * LANES, LANES), :] for c in range(TOGETHER)],
+        [rows[pl.ds(start + c * LANES, LANES), :] for c in range(STRIDE)],
         count_ref,
         conf_ref,
         rating_ref,
@@ -579,16 +586,16 @@
     vmem = pl.BlockSpec(memory_space=pltpu.VMEM)
     smem = pl.BlockSpec(memory_space=pltpu.SMEM)
     hbm = pl.BlockSpec(memory_space=pltpu.HBM)
-    pairs = TOGETHER // 2
+    pairs = STRIDE // 2
     shapes = [
         ((blocks // 2, LANES, 2 * LANES), jnp.bfloat16, pairs),
         ((blocks // 2, 2 * LANES, LANES), jnp.bfloat16, pairs),
-        ((blocks, 8, LANES), jnp.float32, TOGETHER),
-        ((blocks, 8, LANES), jnp.float32, TOGETHER),
+        ((blocks, 8, LANES), jnp.float32, STRIDE),
+        ((blocks, 8, LANES), jnp.float32, STRIDE),
     ]
     return pl.pallas_call(
         build_items_kernel,
-        grid=(blocks // TOGETHER,),
+        grid=(blocks // STRIDE,),
         in_specs=[smem, smem, hbm, vmem, hbm, vmem, vmem],
         out_specs=[
             pl.BlockSpec((step,) + shape[1:], lambda i: (i, 0, 0)) for shape, _, step in shapes
@@ -608,24 +615,30 @@
 
 
 def solve_items_kernel(gram_scale, *refs):
-    built, (gram_ref, table_ref, out_ref, table) = refs[:4], refs[4:8]
-    turned, weighted, inside, x_ref, r_ref, p_ref, g_ref, sems = refs[8:]
+    built, (warm_ref, gram_ref, table_ref, out_ref, table) = refs[:4], refs[4:9]
+    turned, weighted, inside, x_ref, r_ref, p_ref, g_ref, sems = refs[9:]
     loads = [
         pltpu.make_async_copy(source, target, sems.at[k])
         for k, (source, target) in enumerate(zip(built, (turned, weighted, inside, r_ref)))
     ]
     for load in loads:
         load.start()
-    loads.append(pltpu.make_async_copy(table_ref, table, sems.at[4]))
-    loads[4].start()
     batch = 4 * x_ref.shape[0]
     rest = pl.ds(batch, table.shape[0] - batch)
+    fetch = pltpu.make_async_copy(table_ref.at[rest], table.at[rest], sems.at[4])
     keep = pltpu.make_async_copy(table.at[rest], out_ref.at[rest], sems.at[5])
+    start_from(warm_ref, x_ref, p_ref)
     for load in loads:
         load.wait()
-    keep.start()
-    start_from(table, x_ref, p_ref)
-    conjugate(gram_ref[...] * gram_scale, turned, weighted, inside, x_ref, r_ref, p_ref, g_ref)
+    fetch.start()
+
+    def midway():
+        fetch.wait()
+        keep.start()
+
+    conjugate(
+        gram_ref[...] * gram_scale, turned, weighted, inside, x_ref, r_ref, p_ref, g_ref, midway
+    )
     give(x_ref, table)
     first = pl.ds(0, batch)
     put = pltpu.make_async_copy(table.at[first], out_ref.at[first], sems.at[6])
@@ -640,7 +653,7 @@
     hbm = pl.BlockSpec(memory_space=pltpu.HBM)
     return pl.pallas_call(
         functools.partial(solve_items_kernel, gram_scale),
-        in_specs=[hbm] * 4 + [vmem, hbm],
+        in_specs=[hbm] * 4 + [vmem, vmem, hbm],
         out_specs=hbm,
         out_shape=jax.ShapeDtypeStruct(table.shape, jnp.float32),
         scratch_shapes=[pltpu.VMEM(table.shape, jnp.float32)]
@@ -648,7 +661,7 @@
         + [pltpu.SemaphoreType.DMA((7,))],
         compiler_params=pltpu.CompilerParams(vmem_limit_bytes=48 << 20),
         name="solve_items",
-    )(*[hold(x) for x in built], gram, hold(table))
+    )(*[hold(x) for x in built], table[: 4 * blocks], gram, hold(table))
 
 
 def hold(values):

time: 157 us -> 154 us (0.981)
  Pallas kernels: 79.5 us -> 74.5 us
  waiting for transfers between devices: 27.3 us -> 23.8 us
  matrix products: 1.78 us -> 3.94 us
  starting transfers between devices: 21.9 us -> 23.7 us
  local copies, waits for them, and re-layouts: 1.93 us -> 3.52 us
    pallas_call x1, Pallas kernels: 12.2 us -> 8.13 us  [build_items(): pl.pallas_call(build_items_kernel, grid=(blocks // STRIDE,), in_specs=[sm...]
    all_to_all x4, waiting for transfers between devices: 27.3 us -> 23.8 us  [exchange(): return lax.all_to_all(values, AXES, split_axis=0, concat_axis=0, tiled=True)]
    dot_general x1, matrix products: 1.78 us -> 3.94 us  [local_gram(): jnp.dot(table.T, table, precision=lax.Precision.HIGH, preferred_element_t...]
    all_to_all x4, starting transfers between devices: 21.9 us -> 23.7 us  [exchange(): return lax.all_to_all(values, AXES, split_axis=0, concat_axis=0, tiled=True)]
    unnamed x19, local copies, waits for them, and re-layouts: 0.23 us -> 1.81 us
  transfers between devices with their start and end apart: 4 -> 4, of which waited for: 3 -> 4; matrix products, arithmetic and copies ran while one was open for 2% -> 4% of each run, Pallas kernels for 32% -> 31%
where the time goes in v4:
time: 154 us
  Pallas kernels  74.5 us (48%)
  waiting for transfers between devices  23.8 us (15%)
  starting transfers between devices  23.7 us (15%)
  blocking collectives  21.4 us (14%)
  matrix products  3.94 us (3%)
  local copies, waits for them, and re-layouts  3.52 us (2%)
    all_to_all x4, waiting for transfers between devices, exchange(): return lax.all_to_all(values, AXES, split_axis=0, concat_axis=0, tiled=True)  23.8 us
    all_to_all x4, starting transfers between devices, exchange(): return lax.all_to_all(values, AXES, split_axis=0, concat_axis=0, tiled=True)  23.7 us
    pallas_call x1, Pallas kernels, solve_users(): pl.pallas_call(functools.partial(solve_users_kernel, gram_scale), in_spec...  22.3 us
    all_to_all x1, blocking collectives, exchange(): return lax.all_to_all(values, AXES, split_axis=0, concat_axis=0, tiled=True)  21.4 us
    pallas_call x2, Pallas kernels, gather(): pl.pallas_call(functools.partial(gather_kernel, first, count, per_step),...  18.8 us
    pallas_call x1, Pallas kernels, solve_items(): pl.pallas_call(functools.partial(solve_items_kernel, gram_scale), in_spec...  10.6 us
    pallas_call x1, Pallas kernels, build_items(): pl.pallas_call(build_items_kernel, grid=(blocks // STRIDE,), in_specs=[sm...  8.13 us
    pallas_call x1, Pallas kernels, unsort(): pl.pallas_call(unsort_kernel, in_specs=[pl.BlockSpec(memory_space=pltpu.S...  7.77 us
  transfers between devices with their start and end apart: 4, of which 4 were waited for; matrix products, arithmetic and copies ran while one was open for 4% of the time, Pallas kernels for 31%

profile of v4, /device:TPU:1, one launch (start us, length us, event | category | flops | bytes accessed | tf_op | source)
XLA Modules:
  0.0 153.6 jit_solution(13525203136787438834)
XLA Ops:
  0.6 0.0 copy-start
  0.6 6.9 %bucket.1 = (f32[128,256]{1,0:T(8,128)S(1)}, s32[48,128]{1,0:T(8,128)S(1)}, s32[48,128]{1,0:T(8,128)S(1)}, s32[128,128]{1,0:T(8,128)S(1)}) custom-call(s32[48,128]{1,0:T(8,128)} %bitcast.31, s32[48,128]{1,0:T(8,128)} %bitcast.32, s32[48,128]{1,0:T(8,128)} %bitcast.33, s32[48,128]{1,0:T(8,128)} %bitcast.34, f32[4096,128]{1,0:T(8,128)} %refs_6_.1), custom_call_target="tpu_custom_call" | custom-call | tf_op jit(solution)/shard_map/bucket/pallas_call | solution.py:145
  7.6 0.1 copy.18
  7.7 21.4 %all_to_all.37 = f32[128,1,256]{2,1,0:T(1,128)S(1)} all-to-all(f32[128,1,256]{2,1,0:T(1,128)S(1)} %copy.18), channel_id=1, replica_groups=mesh['gx'=16,'gy'=8] {'gx','gy'}, dimensions={0} | all-to-all | bytes 262144 | tf_op jit(solution)/shard_map/all_to_all | solution.py:672
  29.2 0.0 copy-done
  29.2 10.0 %gather_rows.3 = bf16[128,64,128]{2,1,0:T(8,128)(2,1)} custom-call(s32[128,128]{1,0:T(8,128)S(1)} %get-tuple-element.158.request_ref.wanted_ref, f32[4096,128]{1,0:T(8,128)S(1)} %copy-done, f32[1,128]{1,0:T(1,128)S(1)} %bitcast.28), custom_call_target="tpu_custom_call" | custom-call | tf_op jit(solution)/shard_map/gather_rows/pallas_call | solution.py:196
  39.3 5.1 %all-to-all-start.2 = ((bf16[128,64,128]{2,1,0:T(8,128)(2,1)}), bf16[128,64,128]{2,1,0:T(8,128)(2,1)}, u32[]{:S(2)}, u32[]{:S(2)}) async-start(bf16[128,64,128]{2,1,0:T(8,128)(2,1)} %gather_rows.3), calls=%async_computation.2 | async-start | bytes 4194304 | tf_op jit(solution)/shard_map/all_to_all | solution.py:672
  44.4 3.9 %fusion.still_ref = f32[128,128]{1,0:T(8,128)S(1)} fusion(f32[4096,128]{1,0:T(8,128)} %table_ref.5), kind=kOutput, calls=%fused_computation.4 | convolution fusion | flops 383778816 | bytes 2064384 | tf_op jit(solution)/shard_map/dot_general | solution.py:676
  48.3 0.0 copy-start.1
  48.3 1.6 %copy-done.1 = f32[4096,128]{1,0:T(8,128)S(1)} copy-done((f32[4096,128]{1,0:T(8,128)S(1)}, f32[4096,128]{1,0:T(8,128)}, u32[]{:S(2)}) %copy-start.1) | copy-done | bytes 2097176
  49.9 8.7 %gather_rows.2 = bf16[128,48,128]{2,1,0:T(8,128)(2,1)} custom-call(s32[128,128]{1,0:T(8,128)S(1)} %get-tuple-element.158.request_ref.wanted_ref, f32[4096,128]{1,0:T(8,128)S(1)} %copy-done.1), custom_call_target="tpu_custom_call" | custom-call | tf_op jit(solution)/shard_map/gather_rows/pallas_call | solution.py:196
  58.6 0.0 copy-start.6
  58.6 0.0 copy-start.2
  58.6 0.0 copy-start.3
  58.6 16.1 %all-to-all-done.2 = bf16[128,64,128]{2,1,0:T(8,128)(2,1)} async-done(((bf16[128,64,128]{2,1,0:T(8,128)(2,1)}), bf16[128,64,128]{2,1,0:T(8,128)(2,1)}, u32[]{:S(2)}, u32[]{:S(2)}) %all-to-all-start.2) | async-done | bytes 2097184 | tf_op jit(solution)/shard_map/all_to_all | solution.py:672
  74.7 5.4 %all-to-all-start.3 = ((bf16[128,48,128]{2,1,0:T(8,128)(2,1)}), bf16[128,48,128]{2,1,0:T(8,128)(2,1)}, u32[]{:S(2)}, u32[]{:S(2)}) async-start(bf16[128,48,128]{2,1,0:T(8,128)(2,1)} %gather_rows.2), calls=%async_computation.3 | async-start | bytes 3145728 | tf_op jit(solution)/shard_map/all_to_all | solution.py:672
  80.1 0.0 copy-done.6
  80.1 0.1 copy.19.count_ref
  80.2 0.0 copy-done.2
  80.2 0.0 copy-done.3
  80.2 22.3 %solve_users.1 = (f32[4096,128]{1,0:T(8,128)}, bf16[128,16,128]{2,1,0:T(8,128)(2,1)}) custom-call(s32[48,128]{1,0:T(8,128)S(1)} %get-tuple-element.129.slot_ref, s32[128,128]{1,0:T(8,128)S(1)} %get-tuple-element.158.request_ref.wanted_ref, s32[48,4]{1,0:T(8,128)S(1)} %copy.19.count_ref, bf16[8192,128]{1,0:T(8,128)(2,1)} %bitcast.7.reply_ref, ...), custom_call_target="tpu_custom_call" | custom-call | tf_op jit(solution)/shard_map/solve_users/pallas_call | solution.py:485
  102.5 2.3 %all-to-all-done.3 = bf16[128,48,128]{2,1,0:T(8,128)(2,1)} async-done(((bf16[128,48,128]{2,1,0:T(8,128)(2,1)}), bf16[128,48,128]{2,1,0:T(8,128)(2,1)}, u32[]{:S(2)}, u32[]{:S(2)}) %all-to-all-start.3) | async-done | bytes 1572896 | tf_op jit(solution)/shard_map/all_to_all | solution.py:672
  104.8 7.6 %all-to-all-start.4 = ((bf16[128,16,128]{2,1,0:T(8,128)(2,1)}), bf16[128,16,128]{2,1,0:T(8,128)(2,1)S(1)}, u32[]{:S(2)}, u32[]{:S(2)}) async-start(bf16[128,16,128]{2,1,0:T(8,128)(2,1)} %get-tuple-element.137), calls=%async_computation.4 | async-start | bytes 1048576 | tf_op jit(solution)/shard_map/all_to_all | solution.py:672
  112.4 0.8 slice_reduce_fusion
  113.2 0.1 slice_minimum_fusion
  113.3 0.9 slice.50
  114.2 7.8 %unsort_rows.1 = f32[48,128,128]{2,1,0:T(8,128)} custom-call(s32[48,128]{1,0:T(8,128)S(1)} %get-tuple-element.138.slot_ref, bf16[6144,128]{1,0:T(8,128)(2,1)} %bitcast.10.reply_ref), custom_call_target="tpu_custom_call" | custom-call | tf_op jit(solution)/shard_map/unsort_rows/pallas_call | solution.py:226
  122.0 4.2 %all-to-all-done.4 = bf16[128,16,128]{2,1,0:T(8,128)(2,1)S(1)} async-done(((bf16[128,16,128]{2,1,0:T(8,128)(2,1)}), bf16[128,16,128]{2,1,0:T(8,128)(2,1)S(1)}, u32[]{:S(2)}, u32[]{:S(2)}) %all-to-all-start.4) | async-done | bytes 524320 | tf_op jit(solution)/shard_map/all_to_all | solution.py:672
  126.1 0.2 convert_reduce_fusion
  126.3 0.0 copy-start.7
  126.3 0.0 copy-start.4
  126.3 0.0 copy-start.5
  126.3 0.7 while.14
  127.0 0.7 broadcast_in_dim.23
  127.7 5.6 %all-to-all-start.5 = ((f32[128,1,128]{2,1,0:T(1,128)}), f32[128,1,128]{2,1,0:T(1,128)S(1)}, u32[]{:S(2)}, u32[]{:S(2)}) async-start(f32[128,1,128]{2,1,0:T(1,128)} %broadcast_in_dim.23), calls=%async_computation.5 | async-start | bytes 131072 | tf_op jit(solution)/shard_map/all_to_all | solution.py:672
  133.3 0.0 copy-done.7
  133.3 0.1 copy.20.count_ref
  133.4 0.0 copy-done.4
  133.4 0.0 copy-done.5
  133.4 8.1 %build_items.1 = (bf16[24,128,256]{2,1,0:T(8,128)(2,1)}, bf16[24,256,128]{2,1,0:T(8,128)(2,1)}, f32[48,8,128]{2,1,0:T(8,128)}, f32[48,8,128]{2,1,0:T(8,128)}) custom-call(s32[128,128]{1,0:T(8,128)S(1)} %get-tuple-element.134.place_ref, s32[48,4]{1,0:T(8,128)S(1)} %copy.20.count_ref, f32[6144,128]{1,0:T(8,128)} %bitcast.29, bf16[2048,128]{1,0:T(8,128)(2,1)S(1)} %bitcast.21, ...), custom_call_target="tpu_custom_call" | custom-call | tf_op jit(solution)/shard_map/build_items/pallas_call | solution.py:596
  141.6 1.3 all-to-all-done.5
  142.8 10.6 %solve_items.1 = f32[4096,128]{1,0:T(8,128)} custom-call(bf16[24,128,256]{2,1,0:T(8,128)(2,1)} %get-tuple-element.143.refs_0_, bf16[24,256,128]{2,1,0:T(8,128)(2,1)} %get-tuple-element.144.refs_1_, f32[48,8,128]{2,1,0:T(8,128)} %get-tuple-element.145.refs_2_, f32[48,8,128]{2,1,0:T(8,128)} %get-tuple-element.146.refs_3_, f32[192,128]{1,0:T(8,128)S(1)} %slice.33.refs_4_, ...), custom_call_target="tpu_custom_call" | custom-call | tf_op jit(solution)/shard_map/solve_items/pallas_call | solution.py:654
  (3 shorter events, 0.1 us)
Async XLA Ops:
  0.6 28.6 %copy-start = (f32[4096,128]{1,0:T(8,128)S(1)}, f32[4096,128]{1,0:T(8,128)}, u32[]{:S(2)}) copy-start(f32[4096,128]{1,0:T(8,128)} %refs_6_.1) | copy-start | bytes 6291460
  39.3 35.4 %all-to-all-start.2 = ((bf16[128,64,128]{2,1,0:T(8,128)(2,1)}), bf16[128,64,128]{2,1,0:T(8,128)(2,1)}, u32[]{:S(2)}, u32[]{:S(2)}) async-start(bf16[128,64,128]{2,1,0:T(8,128)(2,1)} %gather_rows.3), calls=%async_computation.2 | async-start | bytes 4194304 | tf_op jit(solution)/shard_map/all_to_all | solution.py:672
  48.3 1.6 %copy-start.1 = (f32[4096,128]{1,0:T(8,128)S(1)}, f32[4096,128]{1,0:T(8,128)}, u32[]{:S(2)}) copy-start(f32[4096,128]{1,0:T(8,128)} %table_ref.5) | copy-start | bytes 6291460
  58.6 21.4 %copy-start.6 = (s32[48,4]{0,1:T(4,128)S(1)}, s32[48,4]{0,1:T(4,128)}, u32[]{:S(2)}) copy-start(s32[48,4]{0,1:T(4,128)} %param.20) | copy-start | bytes 2308
  58.6 21.5 %copy-start.2 = (f32[6144]{0:T(1024)S(1)}, f32[6144]{0:T(1024)}, u32[]{:S(2)}) copy-start(f32[6144]{0:T(1024)} %param.18) | copy-start | bytes 73732
  58.6 21.5 %copy-start.3 = (f32[6144]{0:T(1024)S(1)}, f32[6144]{0:T(1024)}, u32[]{:S(2)}) copy-start(f32[6144]{0:T(1024)} %param.19) | copy-start | bytes 73732
  74.7 30.1 %all-to-all-start.3 = ((bf16[128,48,128]{2,1,0:T(8,128)(2,1)}), bf16[128,48,128]{2,1,0:T(8,128)(2,1)}, u32[]{:S(2)}, u32[]{:S(2)}) async-start(bf16[128,48,128]{2,1,0:T(8,128)(2,1)} %gather_rows.2), calls=%async_computation.3 | async-start | bytes 3145728 | tf_op jit(solution)/shard_map/all_to_all | solution.py:672
  104.8 21.3 %all-to-all-start.4 = ((bf16[128,16,128]{2,1,0:T(8,128)(2,1)}), bf16[128,16,128]{2,1,0:T(8,128)(2,1)S(1)}, u32[]{:S(2)}, u32[]{:S(2)}) async-start(bf16[128,16,128]{2,1,0:T(8,128)(2,1)} %get-tuple-element.137), calls=%async_computation.4 | async-start | bytes 1048576 | tf_op jit(solution)/shard_map/all_to_all | solution.py:672
  126.3 7.0 %copy-start.7 = (s32[48,4]{0,1:T(4,128)S(1)}, s32[48,4]{0,1:T(4,128)}, u32[]{:S(2)}) copy-start(s32[48,4]{0,1:T(4,128)} %param.25) | copy-start | bytes 2308
  126.3 7.1 %copy-start.4 = (f32[6144]{0:T(1024)S(1)}, f32[6144]{0:T(1024)}, u32[]{:S(2)}) copy-start(f32[6144]{0:T(1024)} %param.23) | copy-start | bytes 73732
  126.3 7.1 %copy-start.5 = (f32[6144]{0:T(1024)S(1)}, f32[6144]{0:T(1024)}, u32[]{:S(2)}) copy-start(f32[6144]{0:T(1024)} %param.24) | copy-start | bytes 73732
  127.7 15.1 %all-to-all-start.5 = ((f32[128,1,128]{2,1,0:T(1,128)}), f32[128,1,128]{2,1,0:T(1,128)S(1)}, u32[]{:S(2)}, u32[]{:S(2)}) async-start(f32[128,1,128]{2,1,0:T(1,128)} %broadcast_in_dim.23), calls=%async_computation.5 | async-start | bytes 131072 | tf_op jit(solution)/shard_map/all_to_all | solution.py:672

commit v5 on v4

--- a/solution.py
+++ b/solution.py
@@ -198,7 +198,7 @@
         grid=(steps,),
         in_specs=[
             pl.BlockSpec(memory_space=pltpu.SMEM),
-            pl.BlockSpec(table.shape, lambda i: (0, 0)),
+            pl.BlockSpec(memory_space=pltpu.VMEM),
         ]
         + [pl.BlockSpec(extra.shape, lambda i: (0, 0)) for extra in more],
         out_specs=pl.BlockSpec((per_step, depth, LANES), lambda i: (i, 0, 0)),
@@ -306,35 +306,40 @@
         out_ref[pl.ds(4 * b, 4), :] = x_ref[b, :4, :]
 
 
+def local_images(cut, turned, weighted, inside, ids):
+    nought = jnp.zeros((8, LANES), jnp.bfloat16)
+    along = []
+    for c in range(0, len(ids), 2):
+        out = jnp.dot(
+            jnp.concatenate(cut[c : c + 2], 0),
+            turned[ids[c] // 2],
+            preferred_element_type=jnp.float32,
+        )
+        along += [fold(out[:8, :LANES]), fold(out[8:, LANES:])]
+    back = []
+    for c in range(0, len(ids), 2):
+        one, two = [split(along[k] * inside[ids[k]]) for k in (c, c + 1)]
+        both = jnp.concatenate(
+            [jnp.concatenate([one, nought], 1), jnp.concatenate([nought, two], 1)], 0
+        )
+        out = jnp.dot(both, weighted[ids[c] // 2], preferred_element_type=jnp.float32)
+        back += [out[:8], out[8:]]
+    return back
+
+
 def conjugate(gram, turned, weighted, inside, x_ref, r_ref, p_ref, g_ref, midway=None):
     blocks = x_ref.shape[0]
     gram_head = gram.astype(jnp.bfloat16)
     gram_tail = (gram - gram_head.astype(jnp.float32)).astype(jnp.bfloat16)
     gram_both = jnp.concatenate([gram_head, gram_tail], 1)
     group = 24
-    nought = jnp.zeros((8, LANES), jnp.bfloat16)
 
     def apply_system(g):
         ids = [g * group + c for c in range(group)]
         dirs = [p_ref[b] for b in ids]
         cut = [split(d) for d in dirs]
         shared = jnp.dot(jnp.concatenate(cut, 0), gram_both, preferred_element_type=jnp.float32)
-        along = []
-        for c in range(0, group, 2):
-            out = jnp.dot(
-                jnp.concatenate(cut[c : c + 2], 0),
-                turned[ids[c] // 2],
-                preferred_element_type=jnp.float32,
-            )
-            along += [fold(out[:8, :LANES]), fold(out[8:, LANES:])]
-        back = []
-        for c in range(0, group, 2):
-            one, two = [split(along[k] * inside[ids[k]]) for k in (c, c + 1)]
-            both = jnp.concatenate(
-                [jnp.concatenate([one, nought], 1), jnp.concatenate([nought, two], 1)], 0
-            )
-            out = jnp.dot(both, weighted[ids[c] // 2], preferred_element_type=jnp.float32)
-            back += [out[:8], out[8:]]
+        back = local_images(cut, turned, weighted, inside, ids)
         images = []
         for c in range(group):
             part = shared[8 * c : 8 * c + 8]
@@ -344,7 +349,17 @@
         return ids, dirs, images
 
     for g in range(blocks // group):
-        ids, dirs, images = apply_system(g)
+        if midway is None:
+            ids, _, images = apply_system(g)
+        else:
+            ids = [g * group + c for c in range(group)]
+            shared = jnp.dot(
+                jnp.concatenate([split(p_ref[b]) for b in ids], 0),
+                gram_both,
+                preferred_element_type=jnp.float32,
+            )
+            shared = shared[:, :LANES] + shared[:, LANES:]
+            images = [fold(shared[8 * c : 8 * c + 8]) for c in range(group)]
         for c in range(group):
             resid = r_ref[ids[c]] - images[c]
             r_ref[ids[c]] = resid
@@ -352,9 +367,6 @@
             g_ref[ids[c]] = jnp.broadcast_to(
                 jnp.sum(resid * resid, -1, keepdims=True), (8, LANES)
             )
-
-    if midway is not None:
-        midway()
 
     def iterate(i, state):
         for g in range(blocks // group):
@@ -373,7 +385,10 @@
                 g_ref[b] = jnp.broadcast_to(norm_next, (8, LANES))
         return state
 
-    lax.fori_loop(0, ITERS, iterate, 0)
+    lax.fori_loop(0, ITERS // 2, iterate, 0)
+    if midway is not None:
+        midway()
+    lax.fori_loop(ITERS // 2, ITERS, iterate, 0)
 
 
 def solve_users_kernel(
@@ -519,6 +534,7 @@
     more_ref,
     conf_ref,
     rating_ref,
+    warm_ref,
     turned,
     weighted,
     inside,
@@ -579,9 +595,15 @@
         right,
         0,
     )
-
-
-def build_items(places, counts, rows, patch, more, confidence, rating):
+    warm = warm_ref[pl.ds(pl.multiple_of(first * 4, 8), 4 * STRIDE), :]
+    ids = list(range(STRIDE))
+    begin = [jnp.concatenate([warm[4 * c : 4 * c + 4]] * 2, 0) for c in ids]
+    back = local_images([split(x) for x in begin], turned, weighted, inside, ids)
+    for c in ids:
+        right[c] = right[c] - fold(back[c]) - ridge_weight * begin[c]
+
+
+def build_items(places, counts, rows, patch, more, confidence, rating, warm):
     blocks = confidence.shape[0]
     vmem = pl.BlockSpec(memory_space=pltpu.VMEM)
     smem = pl.BlockSpec(memory_space=pltpu.SMEM)
@@ -596,7 +618,7 @@
     return pl.pallas_call(
         build_items_kernel,
         grid=(blocks // STRIDE,),
-        in_specs=[smem, smem, hbm, vmem, hbm, vmem, vmem],
+        in_specs=[smem, smem, hbm, vmem, hbm, vmem, vmem, vmem],
         out_specs=[
             pl.BlockSpec((step,) + shape[1:], lambda i: (i, 0, 0)) for shape, _, step in shapes
         ],
@@ -611,7 +633,7 @@
         ],
         compiler_params=pltpu.CompilerParams(vmem_limit_bytes=48 << 20),
         name="build_items",
-    )(places, counts, hold(rows), patch, hold(more), confidence, rating)
+    )(places, counts, hold(rows), patch, hold(more), confidence, rating, warm)
 
 
 def solve_items_kernel(gram_scale, *refs):
@@ -753,6 +775,7 @@
         more,
         by_block(item_confidence),
         by_block(item_rating),
+        item_table[:batch],
     )
     return (new_users, solve_items(built, item_table, user_gram, gram_scale))
 

time: 154 us -> 153 us (level)
  no operation moved by 1% of the time
where the time goes in v5:
time: 153 us
  Pallas kernels  73.5 us (48%)
  starting transfers between devices  23.6 us (15%)
  waiting for transfers between devices  23.6 us (15%)
  blocking collectives  21.4 us (14%)
  matrix products  3.94 us (3%)
  local copies, waits for them, and re-layouts  3.52 us (2%)
    all_to_all x4, starting transfers between devices, exchange(): return lax.all_to_all(values, AXES, split_axis=0, concat_axis=0, tiled=True)  23.6 us
    all_to_all x4, waiting for transfers between devices, exchange(): return lax.all_to_all(values, AXES, split_axis=0, concat_axis=0, tiled=True)  23.6 us
    pallas_call x1, Pallas kernels, solve_users(): pl.pallas_call(functools.partial(solve_users_kernel, gram_scale), in_spec...  22.3 us
    all_to_all x1, blocking collectives, exchange(): return lax.all_to_all(values, AXES, split_axis=0, concat_axis=0, tiled=True)  21.4 us
    pallas_call x2, Pallas kernels, gather(): pl.pallas_call(functools.partial(gather_kernel, first, count, per_step),...  18.8 us
    pallas_call x1, Pallas kernels, solve_items(): pl.pallas_call(functools.partial(solve_items_kernel, gram_scale), in_spec...  9.34 us
    pallas_call x1, Pallas kernels, build_items(): pl.pallas_call(build_items_kernel, grid=(blocks // STRIDE,), in_specs=[sm...  8.39 us
    pallas_call x1, Pallas kernels, unsort(): pl.pallas_call(unsort_kernel, in_specs=[pl.BlockSpec(memory_space=pltpu.S...  7.77 us
  transfers between devices with their start and end apart: 4, of which 4 were waited for; matrix products, arithmetic and copies ran while one was open for 4% of the time, Pallas kernels for 31%

profile of v5, /device:TPU:1, one launch (start us, length us, event | category | flops | bytes accessed | tf_op | source)
XLA Modules:
  0.0 152.5 jit_solution(4716955375337648335)
XLA Ops:
  0.6 0.0 copy-start
  0.6 6.9 %bucket.1 = (f32[128,256]{1,0:T(8,128)S(1)}, s32[48,128]{1,0:T(8,128)S(1)}, s32[48,128]{1,0:T(8,128)S(1)}, s32[128,128]{1,0:T(8,128)S(1)}) custom-call(s32[48,128]{1,0:T(8,128)} %bitcast.31, s32[48,128]{1,0:T(8,128)} %bitcast.32, s32[48,128]{1,0:T(8,128)} %bitcast.33, s32[48,128]{1,0:T(8,128)} %bitcast.34, f32[4096,128]{1,0:T(8,128)} %refs_6_.1), custom_call_target="tpu_custom_call" | custom-call | tf_op jit(solution)/shard_map/bucket/pallas_call | solution.py:145
  7.6 0.1 copy.18
  7.7 21.4 %all_to_all.37 = f32[128,1,256]{2,1,0:T(1,128)S(1)} all-to-all(f32[128,1,256]{2,1,0:T(1,128)S(1)} %copy.18), channel_id=1, replica_groups=mesh['gx'=16,'gy'=8] {'gx','gy'}, dimensions={0} | all-to-all | bytes 262144 | tf_op jit(solution)/shard_map/all_to_all | solution.py:694
  29.2 0.0 copy-done
  29.2 10.0 %gather_rows.3 = bf16[128,64,128]{2,1,0:T(8,128)(2,1)} custom-call(s32[128,128]{1,0:T(8,128)S(1)} %get-tuple-element.158.request_ref.wanted_ref, f32[4096,128]{1,0:T(8,128)S(1)} %copy-done, f32[1,128]{1,0:T(1,128)S(1)} %bitcast.28), custom_call_target="tpu_custom_call" | custom-call | tf_op jit(solution)/shard_map/gather_rows/pallas_call | solution.py:196
  39.3 5.1 %all-to-all-start.2 = ((bf16[128,64,128]{2,1,0:T(8,128)(2,1)}), bf16[128,64,128]{2,1,0:T(8,128)(2,1)}, u32[]{:S(2)}, u32[]{:S(2)}) async-start(bf16[128,64,128]{2,1,0:T(8,128)(2,1)} %gather_rows.3), calls=%async_computation.2 | async-start | bytes 4194304 | tf_op jit(solution)/shard_map/all_to_all | solution.py:694
  44.4 3.9 %fusion.still_ref = f32[128,128]{1,0:T(8,128)S(1)} fusion(f32[4096,128]{1,0:T(8,128)} %table_ref.5), kind=kOutput, calls=%fused_computation.4 | convolution fusion | flops 383778816 | bytes 2064384 | tf_op jit(solution)/shard_map/dot_general | solution.py:698
  48.3 0.0 copy-start.1
  48.3 1.6 %copy-done.1 = f32[4096,128]{1,0:T(8,128)S(1)} copy-done((f32[4096,128]{1,0:T(8,128)S(1)}, f32[4096,128]{1,0:T(8,128)}, u32[]{:S(2)}) %copy-start.1) | copy-done | bytes 2097176
  49.9 8.7 %gather_rows.2 = bf16[128,48,128]{2,1,0:T(8,128)(2,1)} custom-call(s32[128,128]{1,0:T(8,128)S(1)} %get-tuple-element.158.request_ref.wanted_ref, f32[4096,128]{1,0:T(8,128)S(1)} %copy-done.1), custom_call_target="tpu_custom_call" | custom-call | tf_op jit(solution)/shard_map/gather_rows/pallas_call | solution.py:196
  58.6 0.0 copy-start.6
  58.6 0.0 copy-start.2
  58.6 0.0 copy-start.3
  58.6 16.1 %all-to-all-done.2 = bf16[128,64,128]{2,1,0:T(8,128)(2,1)} async-done(((bf16[128,64,128]{2,1,0:T(8,128)(2,1)}), bf16[128,64,128]{2,1,0:T(8,128)(2,1)}, u32[]{:S(2)}, u32[]{:S(2)}) %all-to-all-start.2) | async-done | bytes 2097184 | tf_op jit(solution)/shard_map/all_to_all | solution.py:694
  74.7 5.4 %all-to-all-start.3 = ((bf16[128,48,128]{2,1,0:T(8,128)(2,1)}), bf16[128,48,128]{2,1,0:T(8,128)(2,1)}, u32[]{:S(2)}, u32[]{:S(2)}) async-start(bf16[128,48,128]{2,1,0:T(8,128)(2,1)} %gather_rows.2), calls=%async_computation.3 | async-start | bytes 3145728 | tf_op jit(solution)/shard_map/all_to_all | solution.py:694
  80.1 0.0 copy-done.6
  80.1 0.1 copy.19.count_ref
  80.2 0.0 copy-done.2
  80.2 0.0 copy-done.3
  80.2 22.3 %solve_users.1 = (f32[4096,128]{1,0:T(8,128)}, bf16[128,16,128]{2,1,0:T(8,128)(2,1)}) custom-call(s32[48,128]{1,0:T(8,128)S(1)} %get-tuple-element.129.slot_ref, s32[128,128]{1,0:T(8,128)S(1)} %get-tuple-element.158.request_ref.wanted_ref, s32[48,4]{1,0:T(8,128)S(1)} %copy.19.count_ref, bf16[8192,128]{1,0:T(8,128)(2,1)} %bitcast.7.reply_ref, ...), custom_call_target="tpu_custom_call" | custom-call | tf_op jit(solution)/shard_map/solve_users/pallas_call | solution.py:500
  102.5 2.3 %all-to-all-done.3 = bf16[128,48,128]{2,1,0:T(8,128)(2,1)} async-done(((bf16[128,48,128]{2,1,0:T(8,128)(2,1)}), bf16[128,48,128]{2,1,0:T(8,128)(2,1)}, u32[]{:S(2)}, u32[]{:S(2)}) %all-to-all-start.3) | async-done | bytes 1572896 | tf_op jit(solution)/shard_map/all_to_all | solution.py:694
  104.8 7.6 %all-to-all-start.4 = ((bf16[128,16,128]{2,1,0:T(8,128)(2,1)}), bf16[128,16,128]{2,1,0:T(8,128)(2,1)S(1)}, u32[]{:S(2)}, u32[]{:S(2)}) async-start(bf16[128,16,128]{2,1,0:T(8,128)(2,1)} %get-tuple-element.137), calls=%async_computation.4 | async-start | bytes 1048576 | tf_op jit(solution)/shard_map/all_to_all | solution.py:694
  112.4 0.8 slice_reduce_fusion
  113.2 0.1 slice_minimum_fusion
  113.3 0.9 slice.51
  114.2 7.8 %unsort_rows.1 = f32[48,128,128]{2,1,0:T(8,128)} custom-call(s32[48,128]{1,0:T(8,128)S(1)} %get-tuple-element.138.slot_ref, bf16[6144,128]{1,0:T(8,128)(2,1)} %bitcast.10.reply_ref), custom_call_target="tpu_custom_call" | custom-call | tf_op jit(solution)/shard_map/unsort_rows/pallas_call | solution.py:226
  122.0 4.2 %all-to-all-done.4 = bf16[128,16,128]{2,1,0:T(8,128)(2,1)S(1)} async-done(((bf16[128,16,128]{2,1,0:T(8,128)(2,1)}), bf16[128,16,128]{2,1,0:T(8,128)(2,1)S(1)}, u32[]{:S(2)}, u32[]{:S(2)}) %all-to-all-start.4) | async-done | bytes 524320 | tf_op jit(solution)/shard_map/all_to_all | solution.py:694
  126.1 0.2 convert_reduce_fusion
  126.3 0.0 copy-start.7
  126.3 0.0 copy-start.4
  126.3 0.0 copy-start.5
  126.3 0.9 while.14
  127.2 0.7 broadcast_in_dim.23
  127.9 5.6 %all-to-all-start.5 = ((f32[128,1,128]{2,1,0:T(1,128)}), f32[128,1,128]{2,1,0:T(1,128)S(1)}, u32[]{:S(2)}, u32[]{:S(2)}) async-start(f32[128,1,128]{2,1,0:T(1,128)} %broadcast_in_dim.23), calls=%async_computation.5 | async-start | bytes 131072 | tf_op jit(solution)/shard_map/all_to_all | solution.py:694
  133.5 0.0 copy-done.7
  133.5 0.1 copy.20.count_ref
  133.6 0.0 copy-done.4
  133.6 0.0 copy-done.5
  133.6 8.4 %build_items.1 = (bf16[24,128,256]{2,1,0:T(8,128)(2,1)}, bf16[24,256,128]{2,1,0:T(8,128)(2,1)}, f32[48,8,128]{2,1,0:T(8,128)}, f32[48,8,128]{2,1,0:T(8,128)}) custom-call(s32[128,128]{1,0:T(8,128)S(1)} %get-tuple-element.134.place_ref, s32[48,4]{1,0:T(8,128)S(1)} %copy.20.count_ref, f32[6144,128]{1,0:T(8,128)} %bitcast.29, bf16[2048,128]{1,0:T(8,128)(2,1)S(1)} %bitcast.21, ...), custom_call_target="tpu_custom_call" | custom-call | tf_op jit(solution)/shard_map/build_items/pallas_call | solution.py:618
  142.0 1.0 all-to-all-done.5
  143.0 9.3 %solve_items.1 = f32[4096,128]{1,0:T(8,128)} custom-call(bf16[24,128,256]{2,1,0:T(8,128)(2,1)} %get-tuple-element.143.refs_0_, bf16[24,256,128]{2,1,0:T(8,128)(2,1)} %get-tuple-element.144.refs_1_, f32[48,8,128]{2,1,0:T(8,128)} %get-tuple-element.145.refs_2_, f32[48,8,128]{2,1,0:T(8,128)} %get-tuple-element.146.refs_3_, ...), custom_call_target="tpu_custom_call" | custom-call | tf_op jit(solution)/shard_map/solve_items/pallas_call | solution.py:676
  (3 shorter events, 0.1 us)
Async XLA Ops:
  0.6 28.6 %copy-start = (f32[4096,128]{1,0:T(8,128)S(1)}, f32[4096,128]{1,0:T(8,128)}, u32[]{:S(2)}) copy-start(f32[4096,128]{1,0:T(8,128)} %refs_6_.1) | copy-start | bytes 6291460
  39.3 35.4 %all-to-all-start.2 = ((bf16[128,64,128]{2,1,0:T(8,128)(2,1)}), bf16[128,64,128]{2,1,0:T(8,128)(2,1)}, u32[]{:S(2)}, u32[]{:S(2)}) async-start(bf16[128,64,128]{2,1,0:T(8,128)(2,1)} %gather_rows.3), calls=%async_computation.2 | async-start | bytes 4194304 | tf_op jit(solution)/shard_map/all_to_all | solution.py:694
  48.3 1.6 %copy-start.1 = (f32[4096,128]{1,0:T(8,128)S(1)}, f32[4096,128]{1,0:T(8,128)}, u32[]{:S(2)}) copy-start(f32[4096,128]{1,0:T(8,128)} %table_ref.5) | copy-start | bytes 6291460
  58.6 21.4 %copy-start.6 = (s32[48,4]{0,1:T(4,128)S(1)}, s32[48,4]{0,1:T(4,128)}, u32[]{:S(2)}) copy-start(s32[48,4]{0,1:T(4,128)} %param.20) | copy-start | bytes 2308
  58.6 21.5 %copy-start.2 = (f32[6144]{0:T(1024)S(1)}, f32[6144]{0:T(1024)}, u32[]{:S(2)}) copy-start(f32[6144]{0:T(1024)} %param.18) | copy-start | bytes 73732
  58.6 21.5 %copy-start.3 = (f32[6144]{0:T(1024)S(1)}, f32[6144]{0:T(1024)}, u32[]{:S(2)}) copy-start(f32[6144]{0:T(1024)} %param.19) | copy-start | bytes 73732
  74.7 30.1 %all-to-all-start.3 = ((bf16[128,48,128]{2,1,0:T(8,128)(2,1)}), bf16[128,48,128]{2,1,0:T(8,128)(2,1)}, u32[]{:S(2)}, u32[]{:S(2)}) async-start(bf16[128,48,128]{2,1,0:T(8,128)(2,1)} %gather_rows.2), calls=%async_computation.3 | async-start | bytes 3145728 | tf_op jit(solution)/shard_map/all_to_all | solution.py:694
  104.8 21.3 %all-to-all-start.4 = ((bf16[128,16,128]{2,1,0:T(8,128)(2,1)}), bf16[128,16,128]{2,1,0:T(8,128)(2,1)S(1)}, u32[]{:S(2)}, u32[]{:S(2)}) async-start(bf16[128,16,128]{2,1,0:T(8,128)(2,1)} %get-tuple-element.137), calls=%async_computation.4 | async-start | bytes 1048576 | tf_op jit(solution)/shard_map/all_to_all | solution.py:694
  126.3 7.2 %copy-start.7 = (s32[48,4]{0,1:T(4,128)S(1)}, s32[48,4]{0,1:T(4,128)}, u32[]{:S(2)}) copy-start(s32[48,4]{0,1:T(4,128)} %param.25) | copy-start | bytes 2308
  126.3 7.3 %copy-start.4 = (f32[6144]{0:T(1024)S(1)}, f32[6144]{0:T(1024)}, u32[]{:S(2)}) copy-start(f32[6144]{0:T(1024)} %param.23) | copy-start | bytes 73732
  126.3 7.3 %copy-start.5 = (f32[6144]{0:T(1024)S(1)}, f32[6144]{0:T(1024)}, u32[]{:S(2)}) copy-start(f32[6144]{0:T(1024)} %param.24) | copy-start | bytes 73732
  127.9 15.1 %all-to-all-start.5 = ((f32[128,1,128]{2,1,0:T(1,128)}), f32[128,1,128]{2,1,0:T(1,128)S(1)}, u32[]{:S(2)}, u32[]{:S(2)}) async-start(f32[128,1,128]{2,1,0:T(1,128)} %broadcast_in_dim.23), calls=%async_computation.5 | async-start | bytes 131072 | tf_op jit(solution)/shard_map/all_to_all | solution.py:694
